TPU v7x, 512 devices: a whole 4x8x8 slice. The times are simulated.
512 devices in a mesh: sec: 8 (over y), rad: 16 (over z, x_hi), ax: 4 (over x_lo, core).
Axes of the slice: x: 4 (x_hi: 2, x_lo: 2; x = x_hi * 2 + x_lo), y: 8, z: 8, core: 2. Of those that a mesh axis runs over, the one named last changes fastest.
Arguments:
- state: float32 [5, 8, 1024, 2048], P(None, 'ax', 'rad', 'sec'), may hold values from -1.6 to 4, as said below
- coarsen: int32 [16], replicated, may hold values from 1 to 16, as said below
Outputs:
- tendency: float32 [5, 8, 1024, 2048], P(None, 'ax', 'rad', 'sec')
Inputs may be any that keep to these rules, and one draw needn't show every extreme that they name: `coarsen`: each entry is a power of two; cycle 0 takes 16 and cycle 16 - 1 takes 1. state[0] (density) lies in 0.6 to 1.4, the momenta in -1.6 to 1.6, state[4] (energy) in 2.5 to 4.0.
All inputs are finite; a program needn't handle non-finite values.
Results may differ from a plain program's by a relative error of at most 0.0003.
Values sent between devices are 32-bit elements; how exact they have to be, the bound alone decides.
A program may use at most 64 MiB of HBM per device.

v0:
```python
import math

import jax
import jax.numpy as jnp
from jax import lax
from jax.sharding import PartitionSpec as P

R_NEAR = 16


GAMMA = 1.4
KAPPA = 1.44


def padded_2(value, sides, width):
    for axis, dim in sides:
        size, length = (lax.axis_size(axis), value.shape[dim])
        up = [(i, (i + 1) % size) for i in range(size)]
        down = [(j, i) for i, j in up]
        last = lax.slice_in_dim(value, length - width, length, axis=dim)
        first = lax.slice_in_dim(value, 0, width, axis=dim)
        before = lax.ppermute(last, axis, up)
        after = lax.ppermute(first, axis, down)
        value = jnp.concatenate([before, value, after], axis=dim)
    return value


def spread(value, axis, root):
    mine = lax.axis_index(axis) == root
    return lax.psum(jnp.where(mine, value, jnp.zeros_like(value)), axis)


def body(state, coarsen):
    fields, planes, cycles_dev, cells_dev = state.shape
    sec_count = lax.axis_size("sec")
    rad_count = lax.axis_size("rad")
    ax_count = lax.axis_size("ax")
    sec_index = lax.axis_index("sec")
    rad_index = lax.axis_index("rad")
    ax_index = lax.axis_index("ax")
    total_cells = cells_dev * sec_count
    dtheta = 2.0 * math.pi / total_cells
    padded = padded_2(state, (("sec", 3), ("rad", 2), ("ax", 1)), 1)
    plane_pos = ax_index * planes + jnp.arange(-1, planes + 1, dtype=jnp.int32)
    cycle_pos = rad_index * cycles_dev + jnp.arange(-1, cycles_dev + 1, dtype=jnp.int32)
    inside_ax = ((plane_pos >= 0) & (plane_pos < planes * ax_count)).astype(jnp.float32)
    inside_rad = ((cycle_pos >= 0) & (cycle_pos < cycles_dev * rad_count)).astype(jnp.float32)
    ghost_plane = jnp.arange(planes + 2) % (planes + 1) == 0
    ghost_cycle = jnp.arange(cycles_dev + 2) % (cycles_dev + 1) == 0
    ghost_cell = jnp.arange(cells_dev + 2) % (cells_dev + 1) == 0
    ghosts = (
        ghost_plane.astype(jnp.int32)[:, None, None]
        + ghost_cycle.astype(jnp.int32)[None, :, None]
        + ghost_cell.astype(jnp.int32)[None, None, :]
    )
    corner = ghosts >= 2
    density = jnp.where(corner, 1.0, padded[0])
    mom_ax = padded[1]
    mom_rad = padded[2]
    mom_az = padded[3]
    energy = padded[4]
    vel_ax = mom_ax / density
    vel_rad = mom_rad / density
    vel_az = mom_az / density
    pressure = (GAMMA - 1.0) * (
        energy - 0.5 * (mom_ax * vel_ax + mom_rad * vel_rad + mom_az * vel_az)
    )
    radius_pad = cycle_pos.astype(jnp.float32) + 0.5
    flux_ax = jnp.stack(
        [
            mom_ax,
            mom_ax * vel_ax + pressure,
            mom_rad * vel_ax,
            mom_az * vel_ax,
            (energy + pressure) * vel_ax,
        ]
    )
    flux_ax = flux_ax * inside_ax[None, :, None, None]
    flux_rad = jnp.stack(
        [
            mom_rad,
            mom_ax * vel_rad,
            mom_rad * vel_rad + pressure,
            mom_az * vel_rad,
            (energy + pressure) * vel_rad,
        ]
    )
    flux_rad = flux_rad * (radius_pad * inside_rad)[None, None, :, None]
    flux_az = jnp.stack(
        [
            mom_az,
            mom_ax * vel_az,
            mom_rad * vel_az,
            mom_az * vel_az + pressure,
            (energy + pressure) * vel_az,
        ]
    )
    radius = radius_pad[1:-1][:, None]
    tendency = -(flux_ax[:, 2:, 1:-1, 1:-1] - flux_ax[:, :-2, 1:-1, 1:-1]) * 0.5
    tendency = (
        tendency - (flux_rad[:, 1:-1, 2:, 1:-1] - flux_rad[:, 1:-1, :-2, 1:-1]) * 0.5 / radius
    )
    tendency = tendency - (flux_az[:, 1:-1, 1:-1, 2:] - flux_az[:, 1:-1, 1:-1, :-2]) * 0.5 / (
        radius * dtheta
    )
    inner_press = pressure[1:-1, 1:-1, 1:-1]
    inner_mom_az = mom_az[1:-1, 1:-1, 1:-1]
    inner_mom_rad = mom_rad[1:-1, 1:-1, 1:-1]
    inner_vel_az = vel_az[1:-1, 1:-1, 1:-1]
    zero_part = jnp.zeros_like(inner_press)
    source = jnp.stack(
        [
            zero_part,
            zero_part,
            (inner_press + inner_mom_az * inner_vel_az) / radius,
            -(inner_mom_rad * inner_vel_az) / radius,
            zero_part,
        ]
    )
    tendency = tendency + source
    own_pos = sec_index * cells_dev + jnp.arange(cells_dev, dtype=jnp.int32)

    def kernel(cycle_factor, cycle_blocks, log_ratio, scale_const, columns):
        rows_coarse = own_pos // cycle_factor
        columns_coarse = columns // cycle_factor
        distance = ((rows_coarse[:, None] - columns_coarse[None, :]) % cycle_blocks).astype(
            jnp.float32
        )
        blocks_f = cycle_blocks.astype(jnp.float32)
        return (jnp.exp(distance * log_ratio) + jnp.exp((blocks_f - distance) * log_ratio)) / (
            scale_const * cycle_factor.astype(jnp.float32)
        )

    near_axis = tendency[:, :, :R_NEAR, :]
    cycle_lines = jnp.transpose(near_axis, (2, 0, 1, 3)).reshape(R_NEAR, fields * planes, cells_dev)
    shared = spread(cycle_lines, "rad", 0)
    per_device = R_NEAR // rad_count
    my_cycles = lax.dynamic_slice_in_dim(shared, rad_index * per_device, per_device, 0)
    selector = (rad_index * per_device + jnp.arange(per_device, dtype=jnp.int32))[
        :, None
    ] == jnp.arange(coarsen.shape[0], dtype=jnp.int32)[None, :]
    factor = jnp.sum(jnp.where(selector, coarsen[None, :], 0), axis=1)
    blocks = total_cells // factor
    factor_f = factor.astype(jnp.float32)
    stiffness = KAPPA / (factor_f * dtheta) ** 2
    inverse_half = 0.5 / stiffness
    one_minus = jnp.sqrt(inverse_half * (2.0 + inverse_half)) - inverse_half
    log_ratio = jnp.log1p(-one_minus)
    scale_const = (
        stiffness
        * one_minus
        * (2.0 - one_minus)
        / (1.0 - one_minus)
        * -jnp.expm1(blocks.astype(jnp.float32) * log_ratio)
    )
    portion = lax.all_gather(my_cycles, "sec", axis=2, tiled=True)
    columns = jnp.arange(portion.shape[2], dtype=jnp.int32)

    def per_cycle(cycle_item):
        lines_one, cycle_factor, cycle_blocks, cycle_log, cycle_scale = cycle_item
        table = kernel(cycle_factor, cycle_blocks, cycle_log, cycle_scale, columns)
        return jnp.einsum("lq,pq->lp", lines_one, table, precision=lax.Precision.HIGHEST)

    smoothed = lax.map(per_cycle, (portion, factor, blocks, log_ratio, scale_const))
    result = lax.all_gather(smoothed, "rad", axis=0, tiled=True)
    restored = jnp.transpose(result.reshape(R_NEAR, fields, planes, cells_dev), (1, 2, 0, 3))
    near_new = jnp.where(rad_index == 0, restored, near_axis)
    return jnp.concatenate([near_new, tendency[:, :, R_NEAR:, :]], axis=2)


def solution(mesh):
    return jax.shard_map(
        body,
        mesh=mesh,
        in_specs=(P(None, "ax", "rad", "sec"), P()),
        out_specs=P(None, "ax", "rad", "sec"),
        check_vma=False,
    )
```

profile of v0, /device:TPU:6, one launch (start us, length us, event | category | flops | bytes accessed | tf_op | source)
XLA Modules:
  0.0 309.1 jit_solution(6789559779002969412)
XLA Ops:
  6.5 1.3 fusion.47
  7.8 3.5 %collective-permute-start = (f32[5,2,64,1]{3,2,1,0:T(8,128)S(1)}, f32[5,2,64,1]{3,2,1,0:T(8,128)S(1)}, u32[]{:S(2)}, u32[]{:S(2)}) collective-permute-start(f32[5,2,64,1]{3,2,1,0:T(8,128)S(1)} %get-tuple-element.59), channel_id=1, source_target_pairs={{0,64},{64,128},{128,192},{192,256},{256,320},{320,384},{384,448},... | collective-permute-start | bytes 7688 | tf_op jit(solution)/shard_map/ppermute | solution.py:22
  11.3 3.8 %collective-permute-start.1 = (f32[5,2,64,1]{3,2,1,0:T(8,128)S(1)}, f32[5,2,64,1]{3,2,1,0:T(8,128)S(1)}, u32[]{:S(2)}, u32[]{:S(2)}) collective-permute-start(f32[5,2,64,1]{3,2,1,0:T(8,128)S(1)} %get-tuple-element.60), channel_id=1, source_target_pairs={{64,0},{128,64},{192,128},{256,192},{320,256},{384,320},{448,384},... | collective-permute-start | bytes 7688 | tf_op jit(solution)/shard_map/ppermute | solution.py:23
  15.2 1.4 fusion.44
  16.6 4.3 %collective-permute-done = f32[5,2,64,1]{3,2,1,0:T(8,128)S(1)} collective-permute-done((f32[5,2,64,1]{3,2,1,0:T(8,128)S(1)}, f32[5,2,64,1]{3,2,1,0:T(8,128)S(1)}, u32[]{:S(2)}, u32[]{:S(2)}) %collective-permute-start) | collective-permute-done | bytes 2592 | tf_op jit(solution)/shard_map/ppermute | solution.py:22
  20.9 1.5 collective-permute-done.1
  22.4 1.1 pad_maximum_fusion.5
  23.5 5.1 %collective-permute-start.2 = (f32[5,2,1,258]{3,2,1,0:T(1,128)S(1)}, f32[5,2,1,258]{3,2,1,0:T(1,128)S(1)}, u32[]{:S(2)}, u32[]{:S(2)}) collective-permute-start(f32[5,2,1,258]{3,2,1,0:T(1,128)S(1)} %get-tuple-element.53), channel_id=1, source_target_pairs={{0,4},{4,8},{8,12},{12,16},{16,20},{20,24},{24,28},{28,32},{32,36}... | collective-permute-start | bytes 30968 | tf_op jit(solution)/shard_map/ppermute | solution.py:22
  28.6 2.2 collective-permute-start.3
  30.9 5.8 %collective-permute-done.3 = f32[5,2,1,258]{3,2,1,0:T(1,128)S(1)} collective-permute-done((f32[5,2,1,258]{3,2,1,0:T(1,128)S(1)}, f32[5,2,1,258]{3,2,1,0:T(1,128)S(1)}, u32[]{:S(2)}, u32[]{:S(2)}) %collective-permute-start.3) | collective-permute-done | bytes 10352 | tf_op jit(solution)/shard_map/ppermute | solution.py:23
  37.2 0.5 copy.5
  37.7 1.9 collective-permute-start.4
  40.2 3.6 %collective-permute-start.5 = (f32[5,1,66,258]{3,1,2,0:T(1,128)S(1)}, f32[5,1,66,258]{3,1,2,0:T(1,128)S(1)}, u32[]{:S(2)}, u32[]{:S(2)}) collective-permute-start(f32[5,1,66,258]{3,1,2,0:T(1,128)S(1)} %copy.6), channel_id=1, source_target_pairs={{1,0},{2,1},{3,2},{0,3},{5,4},{6,5},{7,6},{4,7},{9,8},{10,9},{11,1... | collective-permute-start | bytes 1021688 | tf_op jit(solution)/shard_map/ppermute | solution.py:23
  44.7 6.0 %collective-permute-done.4 = f32[5,1,66,258]{3,1,2,0:T(1,128)S(1)} collective-permute-done((f32[5,1,66,258]{3,1,2,0:T(1,128)S(1)}, f32[5,1,66,258]{3,1,2,0:T(1,128)S(1)}, u32[]{:S(2)}, u32[]{:S(2)}) %collective-permute-start.4) | collective-permute-done | bytes 340592 | tf_op jit(solution)/shard_map/ppermute | solution.py:22
  53.6 1.1 fusion.19
  54.7 0.7 slice_select_fusion.1
  55.4 0.8 and_select_fusion
  58.5 0.8 add_select_fusion.1
  59.4 161.4 %all-reduce.2.cloned.1.call-done = f32[16,10,256]{2,0,1:T(8,128)} async-done(((f32[16,10,256]{2,0,1:T(8,128)}), f32[16,10,256]{2,0,1:T(8,128)}) %all-reduce.2.cloned.1.call-update) | async-done | bytes 163856 | tf_op jit(solution)/shard_map/psum | solution.py:30
  220.8 0.9 constant_dynamic-slice_fusion
  221.7 16.7 %all_gather.6 = f32[1,10,2048]{2,0,1:T(1,128)S(1)} all-gather(f32[1,10,256]{2,0,1:T(1,128)S(1)} %constant_dynamic-slice_fusion), channel_id=1, replica_groups=mesh['sec'=8,'rad'=16,'ax'=4] {'sec'}, dimensions={2}, use_global_device_ids=true | all-gather | bytes 92160 | tf_op jit(solution)/shard_map/all_gather | solution.py:156
  238.4 22.6 %fusion.7 = f32[1,10,256]{2,1,0:T(8,128)S(1)} fusion(f32[]{:T(128)S(6)} %mul.233, f32[]{:T(128)S(6)} %convert_element_type.66, f32[]{:T(128)} %bitcast.13, s32[]{:T(128)S(6)} %select_n.132, s32[2048]{0:T(1024)S(1)} %add_select_fusion.1, s32[256]{0:T(256)S(1)} %and_select_fusion, pred[]{:T(512)S(6)} %lt.63, f32[1,10,2048]{2,0,1:T(1,128)S(1)} %all_gather.6), kind=kOutput, calls=%fused_computation.10 | convolution fusion | flops 70254592 | bytes 101393 | tf_op jit(solution)/shard_map/while/body/eval_jaxpr/lq,pq->lp/dot_general | solution.py:162
  261.0 40.3 %all-gather.1 = f32[16,10,256]{2,1,0:T(8,128)S(1)} all-gather(f32[1,10,256]{2,1,0:T(8,128)S(1)} %fusion.7), channel_id=2, replica_groups=mesh['sec'=8,'rad'=16,'ax'=4] {'rad'}, dimensions={0}, use_global_device_ids=true | all-gather | bytes 174080 | tf_op jit(solution)/shard_map/all_gather | solution.py:165
  301.4 0.9 pad_maximum_fusion.2
  (38 shorter events, 4.4 us)
Async XLA Ops:
  6.5 30.1 %copy-start = (f32[5,2,64,256]{3,2,1,0:T(8,128)S(1)}, f32[5,2,64,256]{3,2,1,0:T(8,128)}, u32[]{:S(2)}) copy-start(f32[5,2,64,256]{3,2,1,0:T(8,128)} %param.2) | copy-start | bytes 1966084
  6.5 214.2 %all-reduce.2.cloned.1.call-start = ((), (), s32[]{:S(2)}) async-start(), calls=%async_computation | async-start | bytes 327680 | tf_op jit(solution)/shard_map/psum | solution.py:30
  7.8 13.1 %collective-permute-start = (f32[5,2,64,1]{3,2,1,0:T(8,128)S(1)}, f32[5,2,64,1]{3,2,1,0:T(8,128)S(1)}, u32[]{:S(2)}, u32[]{:S(2)}) collective-permute-start(f32[5,2,64,1]{3,2,1,0:T(8,128)S(1)} %get-tuple-element.59), channel_id=1, source_target_pairs={{0,64},{64,128},{128,192},{192,256},{256,320},{320,384},{384,448},... | collective-permute-start | bytes 7688 | tf_op jit(solution)/shard_map/ppermute | solution.py:22
  11.3 11.1 %collective-permute-start.1 = (f32[5,2,64,1]{3,2,1,0:T(8,128)S(1)}, f32[5,2,64,1]{3,2,1,0:T(8,128)S(1)}, u32[]{:S(2)}, u32[]{:S(2)}) collective-permute-start(f32[5,2,64,1]{3,2,1,0:T(8,128)S(1)} %get-tuple-element.60), channel_id=1, source_target_pairs={{64,0},{128,64},{192,128},{256,192},{320,256},{384,320},{448,384},... | collective-permute-start | bytes 7688 | tf_op jit(solution)/shard_map/ppermute | solution.py:23
  23.5 7.4 %collective-permute-start.2 = (f32[5,2,1,258]{3,2,1,0:T(1,128)S(1)}, f32[5,2,1,258]{3,2,1,0:T(1,128)S(1)}, u32[]{:S(2)}, u32[]{:S(2)}) collective-permute-start(f32[5,2,1,258]{3,2,1,0:T(1,128)S(1)} %get-tuple-element.53), channel_id=1, source_target_pairs={{0,4},{4,8},{8,12},{12,16},{16,20},{20,24},{24,28},{28,32},{32,36}... | collective-permute-start | bytes 30968 | tf_op jit(solution)/shard_map/ppermute | solution.py:22
  28.6 8.0 %collective-permute-start.3 = (f32[5,2,1,258]{3,2,1,0:T(1,128)S(1)}, f32[5,2,1,258]{3,2,1,0:T(1,128)S(1)}, u32[]{:S(2)}, u32[]{:S(2)}) collective-permute-start(f32[5,2,1,258]{3,2,1,0:T(1,128)S(1)} %get-tuple-element.54), channel_id=1, source_target_pairs={{4,0},{8,4},{12,8},{16,12},{20,16},{24,20},{28,24},{32,28},{36,32}... | collective-permute-start | bytes 30968 | tf_op jit(solution)/shard_map/ppermute | solution.py:23
  37.7 13.0 %collective-permute-start.4 = (f32[5,1,66,258]{3,1,2,0:T(1,128)S(1)}, f32[5,1,66,258]{3,1,2,0:T(1,128)S(1)}, u32[]{:S(2)}, u32[]{:S(2)}) collective-permute-start(f32[5,1,66,258]{3,1,2,0:T(1,128)S(1)} %copy.5), channel_id=1, source_target_pairs={{0,1},{1,2},{2,3},{3,0},{4,5},{5,6},{6,7},{7,4},{8,9},{9,10},{10,1... | collective-permute-start | bytes 1021688 | tf_op jit(solution)/shard_map/ppermute | solution.py:22
  40.2 10.7 %collective-permute-start.5 = (f32[5,1,66,258]{3,1,2,0:T(1,128)S(1)}, f32[5,1,66,258]{3,1,2,0:T(1,128)S(1)}, u32[]{:S(2)}, u32[]{:S(2)}) collective-permute-start(f32[5,1,66,258]{3,1,2,0:T(1,128)S(1)} %copy.6), channel_id=1, source_target_pairs={{1,0},{2,1},{3,2},{0,3},{5,4},{6,5},{7,6},{4,7},{9,8},{10,9},{11,1... | collective-permute-start | bytes 1021688 | tf_op jit(solution)/shard_map/ppermute | solution.py:23
Sparse Core Ops, SparseCore 0:
  55.5 165.2 all-reduce.1
where the time goes:
time: 310 us; the launch traced here: 309 us
  waiting for transfers between devices  179 us (58%)
  blocking collectives  57 us (18%)
  matrix products  22.6 us (7%)
  starting transfers between devices  20.2 us (7%)
  between operations  16.7 us (5%)
  other arithmetic  9.79 us (3%)
  local copies, waits for them, and re-layouts  3.82 us (1%)
    psum x1, waiting for transfers between devices, spread(): return lax.psum(jnp.where(mine, value, jnp.zeros_like(value)), axis)  161 us
    all_gather x1, blocking collectives, body(): result = lax.all_gather(smoothed, 'rad', axis=0, tiled=True)  40.3 us
    dot_general x1, matrix products, per_cycle(): jnp.einsum('lq,pq->lp', lines_one, table, precision=lax.Precision.HIGHEST)  22.6 us
    all_gather x1, blocking collectives, body(): portion = lax.all_gather(my_cycles, 'sec', axis=2, tiled=True)  16.7 us
    ppermute x3, starting transfers between devices, padded_2(): before = lax.ppermute(last, axis, up)  10.5 us
    ppermute x3, waiting for transfers between devices, padded_2(): before = lax.ppermute(last, axis, up)  10.3 us
    ppermute x3, starting transfers between devices, padded_2(): after = lax.ppermute(first, axis, down)  9.68 us
    ppermute x3, waiting for transfers between devices, padded_2(): after = lax.ppermute(first, axis, down)  7.38 us
  transfers between devices with their start and end apart: 7, of which 6 were waited for; matrix products, arithmetic and copies ran while one was open for 1% of the time, Pallas kernels for 0%

commit v1 on v0

v1 whole, which is shorter than its diff:
```python
import functools
import math

import jax
import jax.numpy as jnp
from jax import lax
from jax.experimental import pallas as pl
from jax.experimental.pallas import tpu as pltpu
from jax.sharding import PartitionSpec as P

GAMMA = 1.4
KAPPA = 1.44
NEAR = 16
FACTORS = (1, 2, 4, 8, 16)
SHIFTS = (1, 2, 4, 8, 16, 32, 64)
MESH = pl.DeviceIdType.MESH
CHUNKS = 4


def filter_constants(total_cells):
    dtheta = 2.0 * math.pi / total_cells
    out = {}
    for f in FACTORS:
        beta = KAPPA / (f * dtheta) ** 2
        half = 0.5 / beta
        gap = math.sqrt(half * (2.0 + half)) - half
        out[f] = (1.0 - gap, math.log1p(-gap), 1.0 / (1.0 + 2.0 * beta * gap))
    return out


def primitive(d, mx, mr, mt, e):
    inv = 1.0 / d
    ux, ur, ut = mx * inv, mr * inv, mt * inv
    p = (GAMMA - 1.0) * (e - 0.5 * (mx * ux + mr * ur + mt * ut))
    return ux, ur, ut, p


def by_factor(fv, values):
    out = jnp.full(fv.shape, values[0], jnp.float32)
    for f, v in zip(FACTORS[1:], values[1:]):
        out = jnp.where(fv == f, jnp.float32(v), out)
    return out


def kernel(
    nsec, nrad, nax,
    coarsen_ref, state_ref, out_ref,
    st, fx, rg, hz, ghost, rad_send, rad_recv, sec_send, sec_recv,
    coef_f, coef_b, near_c, near_a, near_b, car_send, car_keep, car_recv,
    load_sem, ax_ssem, ax_rsem, rad_ssem, rad_rsem, sec_ssem, sec_rsem, car_ssem, car_rsem,
):
    fields, planes, rows, cells = st.shape
    total = cells * nsec
    dtheta = 2.0 * math.pi / total
    tiles = rows // 8
    crow = rows // CHUNKS
    sec, rad, ax = lax.axis_index("sec"), lax.axis_index("rad"), lax.axis_index("ax")
    near = rad == 0

    barrier = pltpu.get_barrier_semaphore()

    def greet(where):
        pl.semaphore_signal(barrier, inc=1, device_id=where, device_id_type=MESH)

    sides = ((ax > 0, {"ax": ax - 1}), (ax < nax - 1, {"ax": ax + 1}))
    rads = ((rad > 0, {"rad": rad - 1}), (rad < nrad - 1, {"rad": rad + 1}))
    others = [{"sec": lax.rem(sec + k, nsec)} for k in range(1, nsec)]
    for cond, where in sides + rads:
        pl.when(cond)(functools.partial(greet, where))
    greet(others[0])
    greet(others[-1])

    @pl.when(near)
    def _():
        for where in others[1:-1]:
            greet(where)

    loads = []
    for c in range(CHUNKS):
        part = pl.ds(c * crow, crow)
        copy = pltpu.make_async_copy(state_ref.at[:, :, part, :], st.at[:, :, part, :], load_sem.at[c])
        copy.start()
        loads.append(copy)

    lane = lax.broadcasted_iota(jnp.int32, (8, 128), 1)
    consts = filter_constants(total)

    def factors():
        row16 = lax.broadcasted_iota(jnp.int32, (NEAR, 128), 0)
        fv = jnp.full((NEAR, 128), 1, jnp.int32)
        for i in range(NEAR):
            fv = jnp.where(row16 == i, coarsen_ref[i], fv)
        return fv

    @pl.when(near)
    def _():
        fv = factors()
        lane16 = lax.broadcasted_iota(jnp.int32, (NEAR, 128), 1)
        for n, d in enumerate(SHIFTS):
            step = by_factor(fv, [math.exp(consts[f][1] * (d // f)) if d >= f else 0.0 for f in FACTORS])
            coef_f[n] = jnp.where(lane16 >= d, step, 0.0)
            coef_b[n] = jnp.where(lane16 < 128 - d, step, 0.0)

    count = 2 + (rad > 0).astype(jnp.int32) + (rad < nrad - 1).astype(jnp.int32)
    count = count + (ax > 0).astype(jnp.int32) + (ax < nax - 1).astype(jnp.int32)
    count = count + jnp.where(near, nsec - 3, 0)
    pl.semaphore_wait(barrier, count)

    def ax_copy(side, c):
        part = pl.ds(c * crow, crow)
        return pltpu.make_async_remote_copy(
            src_ref=state_ref.at[:, (planes - 1) if side == 1 else 0, part, :],
            dst_ref=ghost.at[1 - side, :, part, :],
            send_sem=ax_ssem.at[side, c],
            recv_sem=ax_rsem.at[1 - side, c],
            device_id=sides[side][1],
            device_id_type=MESH,
        )

    for c in range(CHUNKS):
        for side in (0, 1):
            pl.when(sides[side][0])(lambda side=side, c=c: ax_copy(side, c).start())

    for copy in loads:
        copy.wait()

    row8 = lax.broadcasted_iota(jnp.int32, (8, cells), 0)

    def radius(t):
        return (rad * rows + t * 8 + row8).astype(jnp.float32) + 0.5

    def fluxes(t, carry):
        first, last = carry
        part = pl.ds(pl.multiple_of(t * 8, 8), 8)
        padded = pl.ds(pl.multiple_of(t * 8 + 8, 8), 8)
        half_r = 0.5 * radius(t)
        for p in range(planes):
            d, mx, mr, mt, e = [st[k, p, part, :] for k in range(fields)]
            ux, ur, ut, pr = primitive(d, mx, mr, mt, e)
            ep = e + pr
            hx = 0.5 * ux
            for k, v in enumerate((0.5 * mx, mx * hx + 0.5 * pr, mr * hx, mt * hx, ep * hx)):
                fx[k, p, part, :] = v
            gr = half_r * ur
            for k, v in enumerate((half_r * mr, mx * gr, mr * gr + half_r * pr, mt * gr, ep * gr)):
                rg[k, p, padded, :] = v
            s = 0.5 / dtheta
            gt = s * ut
            for k, v in enumerate((s * mt, mx * gt, mr * gt, mt * gt + s * pr, ep * gt)):
                hz[k, p, part, :] = v
                slot = (k * planes + p) * tiles + t
                here = lane == slot
                first = jnp.where(here, pltpu.roll(v[:, :128], slot, 1), first)
                last = jnp.where(here, pltpu.roll(v[:, cells - 128:], slot + 1, 1), last)
        return first, last

    zero = jnp.zeros((8, 128), jnp.float32)
    first, last = lax.fori_loop(0, tiles, fluxes, (zero, zero))
    sec_send[0] = first
    sec_send[1] = last

    def sec_copy(side):
        return pltpu.make_async_remote_copy(
            src_ref=sec_send.at[side],
            dst_ref=sec_recv.at[1 - side],
            send_sem=sec_ssem.at[side],
            recv_sem=sec_rsem.at[1 - side],
            device_id=others[-1] if side == 0 else others[0],
            device_id_type=MESH,
        )

    sec_copy(0).start()
    sec_copy(1).start()

    for k in range(fields):
        for p in range(planes):
            slot = k * planes + p
            rad_send[0, slot:slot + 1, :] = rg[k, p, 8:9, :]
            rad_send[1, slot:slot + 1, :] = rg[k, p, rows + 7:rows + 8, :]

    def rad_copy(side):
        return pltpu.make_async_remote_copy(
            src_ref=rad_send.at[side],
            dst_ref=rad_recv.at[1 - side],
            send_sem=rad_ssem.at[side],
            recv_sem=rad_rsem.at[1 - side],
            device_id=rads[side][1],
            device_id_type=MESH,
        )

    for side in (0, 1):
        pl.when(rads[side][0])(lambda side=side: rad_copy(side).start())

    sec_copy(1).wait_recv()
    sec_copy(0).wait_recv()
    for side in (0, 1):
        edge = 7 if side == 0 else rows + 8

        @pl.when(rads[side][0])
        def _():
            rad_copy(1 - side).wait_recv()
            for k in range(fields):
                for p in range(planes):
                    slot = k * planes + p
                    rg[k, p, edge:edge + 1, :] = rad_recv[side, slot:slot + 1, :]

        @pl.when(jnp.logical_not(rads[side][0]))
        def _():
            for k in range(fields):
                for p in range(planes):
                    rg[k, p, edge:edge + 1, :] = jnp.zeros((1, cells), jnp.float32)

    wide = lax.broadcasted_iota(jnp.int32, (rows, cells), 1)
    before = sec_recv[0]
    after = sec_recv[1]
    place = rad * rows + lax.broadcasted_iota(jnp.int32, (rows, cells), 0)
    inv_r = 1.0 / (place.astype(jnp.float32) + 0.5)

    def edges(packed, slot, to):
        column = [pltpu.roll(packed, (to - slot - t) % 128, 1) for t in range(tiles)]
        column = jnp.concatenate(column, axis=0)
        return jnp.concatenate([column, column], axis=1)

    for p in range(planes):
        for k in range(fields):
            h = hz[k, p]
            slot = (k * planes + p) * tiles
            left = jnp.where(wide == 0, edges(before, slot, 0), pltpu.roll(h, 1, 1))
            right = jnp.where(wide == cells - 1, edges(after, slot, 127), pltpu.roll(h, cells - 1, 1))
            v = left - right
            v = v + (rg[k, p, 7:rows + 7, :] - rg[k, p, 9:rows + 9, :])
            if k == 2:
                v = v + (2.0 * dtheta) * hz[3, p]
            if k == 3:
                v = v - (2.0 * dtheta) * hz[2, p]
            v = v * inv_r
            v = v - fx[k, 1] if p == 0 else v + fx[k, 0]
            out_ref[k, p] = v

    def axial(c):
        for side in (0, 1):
            @pl.when(sides[side][0])
            def _():
                ax_copy(1 - side, c).wait_recv()
                part = pl.ds(c * crow, crow)
                d, mx, mr, mt, e = [ghost[side, k, part, :] for k in range(fields)]
                ux, ur, ut, pr = primitive(d, mx, mr, mt, e)
                s = 0.5 if side == 0 else -0.5
                hx = s * ux
                for k, v in enumerate((s * mx, mx * hx + s * pr, mr * hx, mt * hx, (e + pr) * hx)):
                    out_ref[k, side, part, :] += v

    def car_copy(k):
        return pltpu.make_async_remote_copy(
            src_ref=car_send,
            dst_ref=car_recv.at[k],
            send_sem=car_ssem.at[k],
            recv_sem=car_rsem.at[k],
            device_id=others[k - 1],
            device_id_type=MESH,
        )

    def pack_rates():
        half = by_factor(factors(), [math.exp(consts[f][1] * (128 // f)) for f in FACTORS])
        return jnp.where(lane % 2 == 0, half[0:8], half[8:16])

    npack = fields * planes * 2

    axial(0)

    @pl.when(near)
    def _():
        fv = factors()
        lane3 = lax.broadcasted_iota(jnp.int32, (planes, NEAR, 128), 2)
        fv3 = jnp.broadcast_to(fv[None], (planes, NEAR, 128))
        ends, keeps = zero, zero
        for k in range(fields):
            for half in (0, 1):
                x = out_ref[k, :, 0:NEAR, half * 128:(half + 1) * 128]
                for d in (1, 2, 4, 8):
                    swap = jnp.where((lane3 & d) == 0, pltpu.roll(x, 128 - d, 2), pltpu.roll(x, d, 2))
                    x = jnp.where(fv3 > d, 0.5 * (x + swap), x)
                a, b = x, x
                for n, d in enumerate(SHIFTS):
                    a = a + coef_f[n][None] * pltpu.roll(a, d, 2)
                    b = b + coef_b[n][None] * pltpu.roll(b, 128 - d, 2)
                near_c[half, k] = a + b - x
                for p in range(planes):
                    for rt in (0, 1):
                        u = (k * planes + p) * 2 + rt
                        tail = pltpu.roll(a[p, rt * 8:rt * 8 + 8, :], (u + 1) % 128, 1)
                        head = pltpu.roll(b[p, rt * 8:rt * 8 + 8, :], npack + u, 1)
                        if half == 1:
                            ends = jnp.where(lane == u, tail, ends)
                            keeps = jnp.where(lane == npack + u, head, keeps)
                        else:
                            keeps = jnp.where(lane == u, tail, keeps)
                            ends = jnp.where(lane == npack + u, head, ends)
        car_send[...] = ends + pack_rates() * keeps
        car_keep[...] = keeps
        for k in range(1, nsec):
            car_copy(k).start()

    for c in range(1, CHUNKS):
        axial(c)

    @pl.when(near)
    def _():
        rate = pack_rates()
        sector = rate * rate
        power = [jnp.ones_like(sector)]
        for k in range(nsec):
            power.append(power[-1] * sector)
        forward = lane < npack
        total_in = power[nsec - 1] * car_send[...]
        for k in range(1, nsec):
            car_copy(k).wait_recv()
            total_in = total_in + jnp.where(forward, power[k - 1], power[nsec - 1 - k]) * car_recv[k]
        total_in = total_in / (1.0 - power[nsec])
        inner = car_keep[...] + rate * total_in
        fv = factors()
        inv_f = by_factor(fv, [1.0 / f for f in FACTORS])
        logs = by_factor(fv, [consts[f][1] for f in FACTORS])
        scale = by_factor(fv, [consts[f][2] for f in FACTORS])
        lane16 = lax.broadcasted_iota(jnp.int32, (NEAR, 128), 1).astype(jnp.float32)
        block = jnp.floor(lane16 * inv_f)
        grow = scale * jnp.exp(logs * (block + 1.0))
        fall = scale * jnp.exp(logs * (128.0 * inv_f - block))
        for k in range(fields):
            for p in range(planes):
                for rt in (0, 1):
                    u = (k * planes + p) * 2 + rt
                    part = slice(rt * 8, rt * 8 + 8)
                    for half in (0, 1):
                        src_f, src_b = (total_in, inner) if half == 0 else (inner, total_in)
                        cf = jnp.broadcast_to(src_f[:, u:u + 1], (8, 128))
                        cb = jnp.broadcast_to(src_b[:, npack + u:npack + u + 1], (8, 128))
                        w = scale[part] * near_c[half, k, p, part, :] + grow[part] * cf + fall[part] * cb
                        out_ref[k, p, part, half * 128:(half + 1) * 128] = w

        for k in range(1, nsec):
            car_copy(k).wait_send()

    sec_copy(0).wait_send()
    sec_copy(1).wait_send()
    for side in (0, 1):
        pl.when(rads[side][0])(lambda side=side: rad_copy(side).wait_send())
        for c in range(CHUNKS):
            pl.when(sides[side][0])(lambda side=side, c=c: ax_copy(side, c).wait_send())


def body(state, coarsen):
    fields, planes, rows, cells = state.shape
    nsec, nrad, nax = lax.axis_size("sec"), lax.axis_size("rad"), lax.axis_size("ax")
    block = (fields, planes, rows, cells)
    f32 = jnp.float32
    dma = pltpu.SemaphoreType.DMA
    return pl.pallas_call(
        functools.partial(kernel, nsec, nrad, nax),
        out_shape=jax.ShapeDtypeStruct(block, f32),
        in_specs=[
            pl.BlockSpec(memory_space=pltpu.SMEM),
            pl.BlockSpec(memory_space=pltpu.HBM),
        ],
        out_specs=pl.BlockSpec(memory_space=pltpu.VMEM),
        scratch_shapes=[
            pltpu.VMEM(block, f32),
            pltpu.VMEM(block, f32),
            pltpu.VMEM((fields, planes, rows + 16, cells), f32),
            pltpu.VMEM(block, f32),
            pltpu.VMEM((2, fields, rows, cells), f32),
            pltpu.VMEM((2, fields * planes, cells), f32),
            pltpu.VMEM((2, fields * planes, cells), f32),
            pltpu.VMEM((2, 8, 128), f32),
            pltpu.VMEM((2, 8, 128), f32),
            pltpu.VMEM((len(SHIFTS), NEAR, 128), f32),
            pltpu.VMEM((len(SHIFTS), NEAR, 128), f32),
            pltpu.VMEM((2, fields, planes, NEAR, 128), f32),
            pltpu.VMEM((8, 128), f32),
            pltpu.VMEM((8, 128), f32),
            pltpu.VMEM((8, 128), f32),
            pltpu.VMEM((8, 128), f32),
            pltpu.VMEM((nsec, 8, 128), f32),
            dma((CHUNKS,)),
            dma((2, CHUNKS)),
            dma((2, CHUNKS)),
            dma((2,)),
            dma((2,)),
            dma((2,)),
            dma((2,)),
            dma((nsec,)),
            dma((nsec,)),
        ],
        compiler_params=pltpu.CompilerParams(
            collective_id=0, has_side_effects=True, vmem_limit_bytes=32 * 1024 * 1024
        ),
        cost_estimate=pl.CostEstimate(flops=4_000_000, bytes_accessed=2_000_000, transcendentals=0),
    )(coarsen, state)


def solution(mesh):
    return jax.shard_map(
        body,
        mesh=mesh,
        in_specs=(P(None, "ax", "rad", "sec"), P()),
        out_specs=P(None, "ax", "rad", "sec"),
        check_vma=False,
    )
```

time: 310 us -> 25 us (0.08)
  the two profiles are of different devices: /device:TPU:6 before, /device:TPU:2 now
where the time goes in v1:
time: 25 us; the launch traced here: 24.8 us
  Pallas kernels  22.2 us (89%)
  local copies, waits for them, and re-layouts  2.58 us (10%)
    pallas_call x1, Pallas kernels, body(): pl.pallas_call(functools.partial(kernel, nsec, nrad, nax), out_shape=jax....  22.2 us
    unnamed x5, local copies, waits for them, and re-layouts  2.58 us

profile of v1, /device:TPU:2, one launch (start us, length us, event | category | flops | bytes accessed | tf_op | source)
XLA Modules:
  0.0 24.8 jit_solution(3753759064298863349)
XLA Ops:
  0.0 0.0 copy-start
  0.0 1.1 %copy-done = f32[5,2,64,256]{3,2,1,0:T(8,128)S(1)} copy-done((f32[5,2,64,256]{3,2,1,0:T(8,128)S(1)}, f32[5,2,64,256]{3,2,1,0:T(8,128)}, u32[]{:S(2)}) %copy-start) | copy-done | bytes 655384
  1.1 0.0 copy-start.1
  1.1 0.7 %copy-done.1 = s32[16]{0:T(128)S(1)} copy-done((s32[16]{0:T(128)S(1)}, s32[16]{0:T(128)}, u32[]{:S(2)}) %copy-start.1) | copy-done | bytes 88
  1.7 22.2 %shard_map.28 = f32[5,2,64,256]{3,2,1,0:T(8,128)S(1)} custom-call(s32[16]{0:T(128)S(1)} %copy-done.1, f32[5,2,64,256]{3,2,1,0:T(8,128)S(1)} %copy-done), custom_call_target="tpu_custom_call" | custom-call | flops 4000000 | bytes 2000000 | tf_op jit(solution)/shard_map/pallas_call | solution.py:358
  24.0 0.8 %copy.4 = f32[5,2,64,256]{3,2,1,0:T(8,128)} copy(f32[5,2,64,256]{3,2,1,0:T(8,128)S(1)} %shard_map.28) | data formatting | bytes 1310720
Async XLA Ops:
  0.0 1.1 %copy-start = (f32[5,2,64,256]{3,2,1,0:T(8,128)S(1)}, f32[5,2,64,256]{3,2,1,0:T(8,128)}, u32[]{:S(2)}) copy-start(f32[5,2,64,256]{3,2,1,0:T(8,128)} %state_ref.1) | copy-start | bytes 1966084
  1.1 0.7 %copy-start.1 = (s32[16]{0:T(128)S(1)}, s32[16]{0:T(128)}, u32[]{:S(2)}) copy-start(s32[16]{0:T(128)} %coarsen_ref.1) | copy-start | bytes 196

commit v2 on v1

--- a/solution.py
+++ b/solution.py
@@ -46,8 +46,8 @@
     nsec, nrad, nax,
     coarsen_ref, state_ref, out_ref,
     st, fx, rg, hz, ghost, rad_send, rad_recv, sec_send, sec_recv,
-    coef_f, coef_b, near_c, near_a, near_b, car_send, car_keep, car_recv,
-    load_sem, ax_ssem, ax_rsem, rad_ssem, rad_rsem, sec_ssem, sec_rsem, car_ssem, car_rsem,
+    coef_f, coef_b, weigh_f, weigh_b, near_c, packet, keep_ref, inbox,
+    load_sem, ax_ssem, ax_rsem, rad_ssem, rad_rsem, sec_ssem, sec_rsem, packet_ssem, packet_rsem,
 ):
     fields, planes, rows, cells = st.shape
     total = cells * nsec
@@ -74,6 +74,11 @@
     def _():
         for where in others[1:-1]:
             greet(where)
+        for cond, where in sides:
+            @pl.when(cond)
+            def _():
+                for other in others:
+                    greet({**where, **other})
 
     loads = []
     for c in range(CHUNKS):
@@ -100,26 +105,26 @@
             step = by_factor(fv, [math.exp(consts[f][1] * (d // f)) if d >= f else 0.0 for f in FACTORS])
             coef_f[n] = jnp.where(lane16 >= d, step, 0.0)
             coef_b[n] = jnp.where(lane16 < 128 - d, step, 0.0)
-
-    count = 2 + (rad > 0).astype(jnp.int32) + (rad < nrad - 1).astype(jnp.int32)
-    count = count + (ax > 0).astype(jnp.int32) + (ax < nax - 1).astype(jnp.int32)
-    count = count + jnp.where(near, nsec - 3, 0)
-    pl.semaphore_wait(barrier, count)
-
-    def ax_copy(side, c):
-        part = pl.ds(c * crow, crow)
-        return pltpu.make_async_remote_copy(
-            src_ref=state_ref.at[:, (planes - 1) if side == 1 else 0, part, :],
-            dst_ref=ghost.at[1 - side, :, part, :],
-            send_sem=ax_ssem.at[side, c],
-            recv_sem=ax_rsem.at[1 - side, c],
-            device_id=sides[side][1],
-            device_id_type=MESH,
-        )
-
-    for c in range(CHUNKS):
+        fw = jnp.concatenate([fv, fv], axis=1)
+        share = by_factor(fw, [1.0 / f for f in FACTORS])
+        logs = by_factor(fw, [consts[f][1] for f in FACTORS])
+        block = lax.broadcasted_iota(jnp.int32, (NEAR, cells), 1).astype(jnp.float32)
+        block = jnp.floor(block * share)
+        weigh_f[...] = share * jnp.exp(logs * (cells * share - 1.0 - block))
+        weigh_b[...] = share * jnp.exp(logs * block)
         for side in (0, 1):
-            pl.when(sides[side][0])(lambda side=side, c=c: ax_copy(side, c).start())
+            @pl.when(jnp.logical_not(sides[side][0]))
+            def _():
+                inbox[2 * side] = jnp.zeros((nsec, 8, 128), jnp.float32)
+
+    for side in (0, 1):
+        edge = 7 if side == 0 else rows + 8
+
+        @pl.when(jnp.logical_not(rads[side][0]))
+        def _():
+            for k in range(fields):
+                for p in range(planes):
+                    rg[k, p, edge:edge + 1, :] = jnp.zeros((1, cells), jnp.float32)
 
     for copy in loads:
         copy.wait()
@@ -156,6 +161,86 @@
 
     zero = jnp.zeros((8, 128), jnp.float32)
     first, last = lax.fori_loop(0, tiles, fluxes, (zero, zero))
+    npack = fields * planes * 2
+
+    def rhs(k, p, size, left, right, inv_r):
+        part = slice(0, size)
+        v = left - right
+        v = v + (rg[k, p, 7:size + 7, :] - rg[k, p, 9:size + 9, :])
+        if k == 2:
+            v = v + (2.0 * dtheta) * hz[3, p, part, :]
+        if k == 3:
+            v = v - (2.0 * dtheta) * hz[2, p, part, :]
+        v = v * inv_r
+        return v - fx[k, 1, part, :] if p == 0 else v + fx[k, 0, part, :]
+
+    def inverse_radius(size):
+        place = rad * rows + lax.broadcasted_iota(jnp.int32, (size, cells), 0)
+        return 1.0 / (place.astype(jnp.float32) + 0.5)
+
+    @pl.when(near)
+    def _():
+        wide = lax.broadcasted_iota(jnp.int32, (NEAR, cells), 1)
+        inv_r = inverse_radius(NEAR)
+        wf, wb = weigh_f[...], weigh_b[...]
+        pack = zero
+
+        def put(pack, group, u, column):
+            return jnp.where(lane == group * npack + u, jnp.broadcast_to(column, (8, 128)), pack)
+
+        def total(v):
+            return jnp.sum(v[:, :128] + v[:, 128:], axis=1, keepdims=True)
+
+        for k in range(fields):
+            for p in range(planes):
+                h = hz[k, p, 0:NEAR, :]
+                left = jnp.where(wide == 0, 0.0, pltpu.roll(h, 1, 1))
+                right = jnp.where(wide == cells - 1, 0.0, pltpu.roll(h, cells - 1, 1))
+                v = rhs(k, p, NEAR, left, right, inv_r)
+                beside = fx[k, 1, 0:NEAR, :] if p == 0 else -fx[k, 0, 0:NEAR, :]
+                columns = (
+                    total(v * wf), total(v * wb), h[:, cells - 1:], h[:, :1],
+                    total(beside * wf), total(beside * wb),
+                )
+                for rt in (0, 1):
+                    u = (k * planes + p) * 2 + rt
+                    for group, column in enumerate(columns):
+                        pack = put(pack, group, u, column[rt * 8:rt * 8 + 8])
+        packet[...] = pack
+        inbox[1, 0] = pack
+
+    count = (rad > 0).astype(jnp.int32) + (rad < nrad - 1).astype(jnp.int32)
+    beside = (ax > 0).astype(jnp.int32) + (ax < nax - 1).astype(jnp.int32)
+    count = count + jnp.where(near, nsec - 1 + nsec * beside, 2 + beside)
+    pl.semaphore_wait(barrier, count)
+
+    def packet_copy(to, k):
+        where = {"sec": lax.rem(sec + k, nsec), "ax": ax + (to - 1)}
+        return pltpu.make_async_remote_copy(
+            src_ref=packet,
+            dst_ref=inbox.at[2 - to, k],
+            send_sem=packet_ssem.at[to, k],
+            recv_sem=packet_rsem.at[2 - to, k],
+            device_id=where,
+            device_id_type=MESH,
+        )
+
+    far_first = sorted(range(nsec), key=lambda k: -min(k, nsec - k))
+
+    def packets(act):
+        for k in far_first:
+            if k:
+                act(1, k)
+        for side in (0, 1):
+            @pl.when(sides[side][0])
+            def _():
+                for k in far_first:
+                    act(2 * side, k)
+
+    @pl.when(near)
+    def _():
+        packets(lambda to, k: packet_copy(to, k).start())
+
     sec_send[0] = first
     sec_send[1] = last
 
@@ -191,6 +276,21 @@
     for side in (0, 1):
         pl.when(rads[side][0])(lambda side=side: rad_copy(side).start())
 
+    def ax_copy(side, c):
+        part = pl.ds(c * crow, crow)
+        return pltpu.make_async_remote_copy(
+            src_ref=state_ref.at[:, (planes - 1) if side == 1 else 0, part, :],
+            dst_ref=ghost.at[1 - side, :, part, :],
+            send_sem=ax_ssem.at[side, c],
+            recv_sem=ax_rsem.at[1 - side, c],
+            device_id=sides[side][1],
+            device_id_type=MESH,
+        )
+
+    for c in range(CHUNKS):
+        for side in (0, 1):
+            pl.when(sides[side][0])(lambda side=side, c=c: ax_copy(side, c).start())
+
     sec_copy(1).wait_recv()
     sec_copy(0).wait_recv()
     for side in (0, 1):
@@ -204,17 +304,10 @@
                     slot = k * planes + p
                     rg[k, p, edge:edge + 1, :] = rad_recv[side, slot:slot + 1, :]
 
-        @pl.when(jnp.logical_not(rads[side][0]))
-        def _():
-            for k in range(fields):
-                for p in range(planes):
-                    rg[k, p, edge:edge + 1, :] = jnp.zeros((1, cells), jnp.float32)
-
     wide = lax.broadcasted_iota(jnp.int32, (rows, cells), 1)
     before = sec_recv[0]
     after = sec_recv[1]
-    place = rad * rows + lax.broadcasted_iota(jnp.int32, (rows, cells), 0)
-    inv_r = 1.0 / (place.astype(jnp.float32) + 0.5)
+    inv_r = inverse_radius(rows)
 
     def edges(packed, slot, to):
         column = [pltpu.roll(packed, (to - slot - t) % 128, 1) for t in range(tiles)]
@@ -227,15 +320,7 @@
             slot = (k * planes + p) * tiles
             left = jnp.where(wide == 0, edges(before, slot, 0), pltpu.roll(h, 1, 1))
             right = jnp.where(wide == cells - 1, edges(after, slot, 127), pltpu.roll(h, cells - 1, 1))
-            v = left - right
-            v = v + (rg[k, p, 7:rows + 7, :] - rg[k, p, 9:rows + 9, :])
-            if k == 2:
-                v = v + (2.0 * dtheta) * hz[3, p]
-            if k == 3:
-                v = v - (2.0 * dtheta) * hz[2, p]
-            v = v * inv_r
-            v = v - fx[k, 1] if p == 0 else v + fx[k, 0]
-            out_ref[k, p] = v
+            out_ref[k, p] = rhs(k, p, rows, left, right, inv_r)
 
     def axial(c):
         for side in (0, 1):
@@ -250,22 +335,6 @@
                 for k, v in enumerate((s * mx, mx * hx + s * pr, mr * hx, mt * hx, (e + pr) * hx)):
                     out_ref[k, side, part, :] += v
 
-    def car_copy(k):
-        return pltpu.make_async_remote_copy(
-            src_ref=car_send,
-            dst_ref=car_recv.at[k],
-            send_sem=car_ssem.at[k],
-            recv_sem=car_rsem.at[k],
-            device_id=others[k - 1],
-            device_id_type=MESH,
-        )
-
-    def pack_rates():
-        half = by_factor(factors(), [math.exp(consts[f][1] * (128 // f)) for f in FACTORS])
-        return jnp.where(lane % 2 == 0, half[0:8], half[8:16])
-
-    npack = fields * planes * 2
-
     axial(0)
 
     @pl.when(near)
@@ -273,7 +342,7 @@
         fv = factors()
         lane3 = lax.broadcasted_iota(jnp.int32, (planes, NEAR, 128), 2)
         fv3 = jnp.broadcast_to(fv[None], (planes, NEAR, 128))
-        ends, keeps = zero, zero
+        keeps = zero
         for k in range(fields):
             for half in (0, 1):
                 x = out_ref[k, :, 0:NEAR, half * 128:(half + 1) * 128]
@@ -288,37 +357,51 @@
                 for p in range(planes):
                     for rt in (0, 1):
                         u = (k * planes + p) * 2 + rt
-                        tail = pltpu.roll(a[p, rt * 8:rt * 8 + 8, :], (u + 1) % 128, 1)
-                        head = pltpu.roll(b[p, rt * 8:rt * 8 + 8, :], npack + u, 1)
-                        if half == 1:
-                            ends = jnp.where(lane == u, tail, ends)
+                        if half == 0:
+                            tail = pltpu.roll(a[p, rt * 8:rt * 8 + 8, :], (u + 1) % 128, 1)
+                            keeps = jnp.where(lane == u, tail, keeps)
+                        else:
+                            head = pltpu.roll(b[p, rt * 8:rt * 8 + 8, :], npack + u, 1)
                             keeps = jnp.where(lane == npack + u, head, keeps)
-                        else:
-                            keeps = jnp.where(lane == u, tail, keeps)
-                            ends = jnp.where(lane == npack + u, head, ends)
-        car_send[...] = ends + pack_rates() * keeps
-        car_keep[...] = keeps
-        for k in range(1, nsec):
-            car_copy(k).start()
+        keep_ref[...] = keeps
 
     for c in range(1, CHUNKS):
         axial(c)
 
     @pl.when(near)
     def _():
-        rate = pack_rates()
-        sector = rate * rate
-        power = [jnp.ones_like(sector)]
-        for k in range(nsec):
-            power.append(power[-1] * sector)
-        forward = lane < npack
-        total_in = power[nsec - 1] * car_send[...]
-        for k in range(1, nsec):
-            car_copy(k).wait_recv()
-            total_in = total_in + jnp.where(forward, power[k - 1], power[nsec - 1 - k]) * car_recv[k]
-        total_in = total_in / (1.0 - power[nsec])
-        inner = car_keep[...] + rate * total_in
         fv = factors()
+        packed = jnp.where(lane % 2 == 0, fv[0:8], fv[8:16])
+        rate = by_factor(packed, [math.exp(consts[f][1] * (128 // f)) for f in FACTORS])
+
+        def by_distance(m):
+            logs = [consts[f][1] * (cells // f) for f in FACTORS]
+            return by_factor(packed, [math.exp(g * (m - 1)) / -math.expm1(g * nsec) for g in logs])
+
+        ahead = [None] + [by_distance(m) for m in range(1, nsec + 1)]
+        back = [None] + [ahead[nsec - m] for m in range(1, nsec)] + [ahead[nsec]]
+        row = (lane % 2) * 8 + lax.broadcasted_iota(jnp.int32, (8, 128), 0)
+        edge = by_factor(packed, [1.0 / f for f in FACTORS]) / (row.astype(jnp.float32) + 0.5)
+        across = edge * by_factor(packed, [math.exp(consts[f][1] * (cells // f - 1)) for f in FACTORS])
+        group = lane // npack
+        sum_f, sum_b, sum_x = zero, zero, zero
+        packets(lambda to, k: packet_copy(2 - to, k).wait_recv())
+        for m in range(1, nsec + 1):
+            k = m % nsec
+            prev, after_m = (m - 1) or nsec, m % nsec + 1
+            own = inbox[1, k]
+            sum_f += own * jnp.where(group == 0, ahead[m], jnp.where(group == 2, across * ahead[prev], -edge * ahead[after_m]))
+            sum_b += own * jnp.where(group == 1, back[m], jnp.where(group == 2, edge * back[prev], -across * back[after_m]))
+            both = jnp.where(lane % 4 < 2, inbox[0, k], inbox[2, k])
+            sum_x += both * jnp.where(group == 4, ahead[m], back[m])
+
+        def down(v, groups):
+            return pltpu.roll(v, 128 - groups * npack, 1)
+
+        sum_f = sum_f + down(sum_f, 2) + down(sum_f, 3)
+        sum_b = sum_b + down(sum_b, 1) + down(sum_b, 2)
+        total_in = jnp.where(group == 0, sum_f, sum_b) + down(sum_x, 4)
+        inner = keep_ref[...] + rate * total_in
         inv_f = by_factor(fv, [1.0 / f for f in FACTORS])
         logs = by_factor(fv, [consts[f][1] for f in FACTORS])
         scale = by_factor(fv, [consts[f][2] for f in FACTORS])
@@ -338,8 +421,7 @@
                         w = scale[part] * near_c[half, k, p, part, :] + grow[part] * cf + fall[part] * cb
                         out_ref[k, p, part, half * 128:(half + 1) * 128] = w
 
-        for k in range(1, nsec):
-            car_copy(k).wait_send()
+        packets(lambda to, k: packet_copy(to, k).wait_send())
 
     sec_copy(0).wait_send()
     sec_copy(1).wait_send()
@@ -357,7 +439,7 @@
     dma = pltpu.SemaphoreType.DMA
     return pl.pallas_call(
         functools.partial(kernel, nsec, nrad, nax),
-        out_shape=jax.ShapeDtypeStruct(block, f32),
+        out_shape=pltpu.VMEM(block, f32),
         in_specs=[
             pl.BlockSpec(memory_space=pltpu.SMEM),
             pl.BlockSpec(memory_space=pltpu.HBM),
@@ -375,12 +457,12 @@
             pltpu.VMEM((2, 8, 128), f32),
             pltpu.VMEM((len(SHIFTS), NEAR, 128), f32),
             pltpu.VMEM((len(SHIFTS), NEAR, 128), f32),
+            pltpu.VMEM((NEAR, cells), f32),
+            pltpu.VMEM((NEAR, cells), f32),
             pltpu.VMEM((2, fields, planes, NEAR, 128), f32),
             pltpu.VMEM((8, 128), f32),
             pltpu.VMEM((8, 128), f32),
-            pltpu.VMEM((8, 128), f32),
-            pltpu.VMEM((8, 128), f32),
-            pltpu.VMEM((nsec, 8, 128), f32),
+            pltpu.VMEM((3, nsec, 8, 128), f32),
             dma((CHUNKS,)),
             dma((2, CHUNKS)),
             dma((2, CHUNKS)),
@@ -388,14 +470,14 @@
             dma((2,)),
             dma((2,)),
             dma((2,)),
-            dma((nsec,)),
-            dma((nsec,)),
+            dma((3, nsec)),
+            dma((3, nsec)),
         ],
         compiler_params=pltpu.CompilerParams(
             collective_id=0, has_side_effects=True, vmem_limit_bytes=32 * 1024 * 1024
         ),
         cost_estimate=pl.CostEstimate(flops=4_000_000, bytes_accessed=2_000_000, transcendentals=0),
-    )(coarsen, state)
+    )(pltpu.with_memory_space_constraint(coarsen, pltpu.HBM), pltpu.with_memory_space_constraint(state, pltpu.HBM))
 
 
 def solution(mesh):

time: 25 us -> 18.1 us (0.72)
  the two profiles are of different devices: /device:TPU:2 before, /device:TPU:1 now
where the time goes in v2:
time: 18.1 us; the launch traced here: 18 us
  Pallas kernels  17.1 us (94%)
  local copies, waits for them, and re-layouts  0.84 us (5%)
    pallas_call x1, Pallas kernels, body(): pl.pallas_call(functools.partial(kernel, nsec, nrad, nax), out_shape=pltp...  17.1 us
    unnamed x1, local copies, waits for them, and re-layouts  0.84 us

profile of v2, /device:TPU:1, one launch (start us, length us, event | category | flops | bytes accessed | tf_op | source)
XLA Modules:
  0.0 18.0 jit_solution(6815735113698561137)
XLA Ops:
  0.0 17.1 %shard_map.28 = f32[5,2,64,256]{3,2,1,0:T(8,128)S(1)} custom-call(s32[16]{0:T(128)} %coarsen_ref.1, f32[5,2,64,256]{3,2,1,0:T(8,128)} %state_ref.1), custom_call_target="tpu_custom_call" | custom-call | flops 4000000 | bytes 2000000 | tf_op jit(solution)/shard_map/pallas_call | solution.py:440
  17.1 0.8 %copy.4 = f32[5,2,64,256]{3,2,1,0:T(8,128)} copy(f32[5,2,64,256]{3,2,1,0:T(8,128)S(1)} %shard_map.28) | data formatting | bytes 1310720

commit v3 on v2

--- a/solution.py
+++ b/solution.py
@@ -44,10 +44,11 @@
 
 def kernel(
     nsec, nrad, nax,
-    coarsen_ref, state_ref, out_ref,
-    st, fx, rg, hz, ghost, rad_send, rad_recv, sec_send, sec_recv,
-    coef_f, coef_b, weigh_f, weigh_b, near_c, packet, keep_ref, inbox,
+    coarsen_hbm, state_ref, out_ref,
+    coarsen_ref, coarsen_sem, st, fx, rg, hz, ghost, rad_send, rad_recv, sec_send, sec_recv,
+    coef_f, coef_b, weigh_f, weigh_b, spread, rate_ref, weights, near_c, packet, keep_ref, inbox,
     load_sem, ax_ssem, ax_rsem, rad_ssem, rad_rsem, sec_ssem, sec_rsem, packet_ssem, packet_rsem,
+    ax_ready, rad_ready, sec_ready, packet_ready,
 ):
     fields, planes, rows, cells = st.shape
     total = cells * nsec
@@ -57,29 +58,6 @@
     sec, rad, ax = lax.axis_index("sec"), lax.axis_index("rad"), lax.axis_index("ax")
     near = rad == 0
 
-    barrier = pltpu.get_barrier_semaphore()
-
-    def greet(where):
-        pl.semaphore_signal(barrier, inc=1, device_id=where, device_id_type=MESH)
-
-    sides = ((ax > 0, {"ax": ax - 1}), (ax < nax - 1, {"ax": ax + 1}))
-    rads = ((rad > 0, {"rad": rad - 1}), (rad < nrad - 1, {"rad": rad + 1}))
-    others = [{"sec": lax.rem(sec + k, nsec)} for k in range(1, nsec)]
-    for cond, where in sides + rads:
-        pl.when(cond)(functools.partial(greet, where))
-    greet(others[0])
-    greet(others[-1])
-
-    @pl.when(near)
-    def _():
-        for where in others[1:-1]:
-            greet(where)
-        for cond, where in sides:
-            @pl.when(cond)
-            def _():
-                for other in others:
-                    greet({**where, **other})
-
     loads = []
     for c in range(CHUNKS):
         part = pl.ds(c * crow, crow)
@@ -87,6 +65,113 @@
         copy.start()
         loads.append(copy)
 
+    factor_load = pltpu.make_async_copy(coarsen_hbm, coarsen_ref, coarsen_sem)
+    pl.when(near)(factor_load.start)
+
+    def slow(s, r, a):
+        return (s == 0) & (r == 0) & (a == 0)
+
+    def rank(s, a):
+        turn = jnp.where(s < nsec // 2, s, nsec + nsec // 2 - 1 - s)
+        step = jnp.where(a == 0, 3, jnp.where(a == 1, 0, jnp.where(a == 2, 2, 1)))
+        return 4 * turn + step + jnp.where(slow(s, rad, a), 1000, 0)
+
+    mine = rank(sec, ax)
+    barrier = pltpu.get_barrier_semaphore()
+
+    def signal(sem, where):
+        pl.semaphore_signal(sem, inc=1, device_id=where, device_id_type=MESH)
+
+    sides = [
+        (there, {"ax": a}, there & (rank(sec, a) < mine), there & (rank(sec, a) > mine), there & slow(sec, rad, a))
+        for there, a in ((ax > 0, ax - 1), (ax < nax - 1, ax + 1))
+    ]
+    rads = [
+        (rad > 0, {"rad": rad - 1}, (rad > 0) & ~slow(sec, rad - 1, ax), slow(sec, rad - 1, ax)),
+        (rad < nrad - 1, {"rad": rad + 1}, slow(sec, rad, ax), (rad < nrad - 1) & ~slow(sec, rad, ax)),
+    ]
+    secs = [
+        (True, {"sec": s}, rank(s, ax) < mine, rank(s, ax) > mine)
+        for s in (lax.rem(sec + nsec - 1, nsec), lax.rem(sec + 1, nsec))
+    ]
+    far = ~near
+    for _, where, _, later, *_ in rads + sides:
+        pl.when(later)(functools.partial(signal, barrier, where))
+    for _, where, _, later in secs:
+        pl.when(far & later)(functools.partial(signal, barrier, where))
+
+    tardy = slow(sec, rad, ax)
+    turn = jnp.where(sec < nsec // 2, sec, nsec + nsec // 2 - 1 - sec)
+    reach = near & (ax <= 1) & (sec != 0)
+
+    def span(to, earlier):
+        if not earlier:
+            return jnp.where(tardy, nsec, turn + 1), nsec
+        return jnp.where(tardy | (ax + to == 1), 1, 0), jnp.where(tardy, nsec, turn)
+
+    def there(to):
+        return near if to == 1 else near & sides[to // 2][0]
+
+    def size(to, earlier):
+        lo, hi = span(to, earlier)
+        return jnp.where(there(to), jnp.maximum(hi - lo, 0), 0)
+
+    def visit(earlier, act):
+        for to in (1, 0, 2):
+            def step(t, carry):
+                s = jnp.where(t < nsec // 2, t, nsec + nsec // 2 - 1 - t)
+                act(to, s, ax + (to - 1))
+                return carry
+
+            @pl.when(there(to))
+            def _():
+                lax.fori_loop(*span(to, earlier), step, 0)
+
+    visit(False, lambda to, s, a: signal(barrier, {"sec": s, "ax": a}))
+    pl.when(reach)(lambda: signal(barrier, {"sec": 0, "ax": 0}))
+
+    def number(flags):
+        return sum(jnp.where(flag, 1, 0) for flag in flags)
+
+    count = number(v[2] for v in rads + sides)
+    count = count + jnp.where(near, sum(size(to, True) for to in range(3)), number(v[2] for v in secs))
+    pl.when(count > 0)(lambda: pl.semaphore_wait(barrier, count))
+
+    for ready, pairs in ((ax_ready, sides), (sec_ready, secs), (rad_ready, rads)):
+        for side in (0, 1):
+            pl.when(pairs[side][2])(functools.partial(signal, ready.at[1 - side], pairs[side][1]))
+
+    visit(True, lambda to, s, a: signal(packet_ready.at[jnp.where(tardy, 1, 0)], {"sec": s, "ax": a}))
+
+    def ax_copy(side, c):
+        part = pl.ds(c * crow, crow)
+        return pltpu.make_async_remote_copy(
+            src_ref=state_ref.at[:, (planes - 1) if side == 1 else 0, part, :],
+            dst_ref=ghost.at[1 - side, :, part, :],
+            send_sem=ax_ssem.at[side, c],
+            recv_sem=ax_rsem.at[1 - side, c],
+            device_id=sides[side][1],
+            device_id_type=MESH,
+        )
+
+    def answered(ready, send):
+        pl.semaphore_wait(ready, 1)
+        send()
+
+    def send_ax(side, chunks):
+        for c in chunks:
+            ax_copy(side, c).start()
+
+    head, tail = range(4), range(4, CHUNKS)
+    odd = ax % 2
+    for side in (0, 1):
+        pl.when(sides[side][2] & (odd != side))(functools.partial(send_ax, side, range(CHUNKS)))
+        pl.when(sides[side][2] & (odd == side))(functools.partial(send_ax, side, head))
+    for side in (0, 1):
+        pl.when(sides[side][3] & (odd == side))(
+            lambda side=side: answered(ax_ready.at[side], functools.partial(send_ax, side, head))
+        )
+
     lane = lax.broadcasted_iota(jnp.int32, (8, 128), 1)
     consts = filter_constants(total)
 
@@ -99,6 +184,7 @@
 
     @pl.when(near)
     def _():
+        factor_load.wait()
         fv = factors()
         lane16 = lax.broadcasted_iota(jnp.int32, (NEAR, 128), 1)
         for n, d in enumerate(SHIFTS):
@@ -112,19 +198,39 @@
         block = jnp.floor(block * share)
         weigh_f[...] = share * jnp.exp(logs * (cells * share - 1.0 - block))
         weigh_b[...] = share * jnp.exp(logs * block)
+        scale = by_factor(fv, [consts[f][2] for f in FACTORS])
+        share, logs, block = share[:, :128], logs[:, :128], block[:, :128]
+        spread[0] = scale * jnp.exp(logs * (block + 1.0))
+        spread[1] = scale * jnp.exp(logs * (128.0 * share - block))
+        spread[2] = scale
+        packed = jnp.where(lane % 2 == 0, fv[0:8], fv[8:16])
+        rate_ref[...] = by_factor(packed, [math.exp(consts[f][1] * (128 // f)) for f in FACTORS])
+
+        def by_distance(m):
+            logs = [consts[f][1] * (cells // f) for f in FACTORS]
+            return by_factor(packed, [math.exp(g * (m - 1)) / -math.expm1(g * nsec) for g in logs])
+
+        ahead = [None] + [by_distance(m) for m in range(1, nsec + 1)]
+        back = [None] + [ahead[nsec - m] for m in range(1, nsec)] + [ahead[nsec]]
+        row = (lane % 2) * 8 + lax.broadcasted_iota(jnp.int32, (8, 128), 0)
+        edge = by_factor(packed, [1.0 / f for f in FACTORS]) / (row.astype(jnp.float32) + 0.5)
+        across = edge * by_factor(packed, [math.exp(consts[f][1] * (cells // f - 1)) for f in FACTORS])
+        group = lane // (fields * planes * 2)
+        for m in range(1, nsec + 1):
+            prev, after_m = (m - 1) or nsec, m % nsec + 1
+            k = m % nsec
+            weights[0, k] = jnp.where(group == 0, ahead[m], jnp.where(group == 2, across * ahead[prev], -edge * ahead[after_m]))
+            weights[1, k] = jnp.where(group == 1, back[m], jnp.where(group == 2, edge * back[prev], -across * back[after_m]))
+            weights[2, k] = jnp.where(group == 4, ahead[m], back[m])
         for side in (0, 1):
             @pl.when(jnp.logical_not(sides[side][0]))
             def _():
                 inbox[2 * side] = jnp.zeros((nsec, 8, 128), jnp.float32)
 
-    for side in (0, 1):
-        edge = 7 if side == 0 else rows + 8
-
-        @pl.when(jnp.logical_not(rads[side][0]))
-        def _():
-            for k in range(fields):
-                for p in range(planes):
-                    rg[k, p, edge:edge + 1, :] = jnp.zeros((1, cells), jnp.float32)
+    for k in range(fields):
+        for p in range(planes):
+            for edge in (7, rows + 8):
+                rg[k, p, edge:edge + 1, :] = jnp.zeros((1, cells), jnp.float32)
 
     for copy in loads:
         copy.wait()
@@ -163,9 +269,11 @@
     first, last = lax.fori_loop(0, tiles, fluxes, (zero, zero))
     npack = fields * planes * 2
 
-    def rhs(k, p, size, left, right, inv_r):
+    def rhs(k, p, size, inv_r):
         part = slice(0, size)
-        v = left - right
+        wide = lax.broadcasted_iota(jnp.int32, (size, cells), 1)
+        h = hz[k, p, part, :]
+        v = jnp.where(wide == 0, 0.0, pltpu.roll(h, 1, 1)) - jnp.where(wide == cells - 1, 0.0, pltpu.roll(h, cells - 1, 1))
         v = v + (rg[k, p, 7:size + 7, :] - rg[k, p, 9:size + 9, :])
         if k == 2:
             v = v + (2.0 * dtheta) * hz[3, p, part, :]
@@ -180,7 +288,6 @@
 
     @pl.when(near)
     def _():
-        wide = lax.broadcasted_iota(jnp.int32, (NEAR, cells), 1)
         inv_r = inverse_radius(NEAR)
         wf, wb = weigh_f[...], weigh_b[...]
         pack = zero
@@ -194,9 +301,7 @@
         for k in range(fields):
             for p in range(planes):
                 h = hz[k, p, 0:NEAR, :]
-                left = jnp.where(wide == 0, 0.0, pltpu.roll(h, 1, 1))
-                right = jnp.where(wide == cells - 1, 0.0, pltpu.roll(h, cells - 1, 1))
-                v = rhs(k, p, NEAR, left, right, inv_r)
+                v = rhs(k, p, NEAR, inv_r)
                 beside = fx[k, 1, 0:NEAR, :] if p == 0 else -fx[k, 0, 0:NEAR, :]
                 columns = (
                     total(v * wf), total(v * wb), h[:, cells - 1:], h[:, :1],
@@ -209,37 +314,33 @@
         packet[...] = pack
         inbox[1, 0] = pack
 
-    count = (rad > 0).astype(jnp.int32) + (rad < nrad - 1).astype(jnp.int32)
-    beside = (ax > 0).astype(jnp.int32) + (ax < nax - 1).astype(jnp.int32)
-    count = count + jnp.where(near, nsec - 1 + nsec * beside, 2 + beside)
-    pl.semaphore_wait(barrier, count)
-
-    def packet_copy(to, k):
-        where = {"sec": lax.rem(sec + k, nsec), "ax": ax + (to - 1)}
+    def packet_copy(to, s, a):
         return pltpu.make_async_remote_copy(
             src_ref=packet,
-            dst_ref=inbox.at[2 - to, k],
-            send_sem=packet_ssem.at[to, k],
-            recv_sem=packet_rsem.at[2 - to, k],
-            device_id=where,
+            dst_ref=inbox.at[2 - to, lax.rem(s - sec + nsec, nsec)],
+            send_sem=packet_ssem.at[to],
+            recv_sem=packet_rsem.at[2 - to],
+            device_id={"sec": s, "ax": a},
             device_id_type=MESH,
         )
 
-    far_first = sorted(range(nsec), key=lambda k: -min(k, nsec - k))
-
-    def packets(act):
-        for k in far_first:
-            if k:
-                act(1, k)
-        for side in (0, 1):
-            @pl.when(sides[side][0])
-            def _():
-                for k in far_first:
-                    act(2 * side, k)
-
-    @pl.when(near)
-    def _():
-        packets(lambda to, k: packet_copy(to, k).start())
+    def packet_to(to, s, a):
+        packet_copy(to, s, a).start()
+
+    def all_packets(to):
+        box = inbox.at[to] if to != 1 else inbox.at[1, pl.ds(1, nsec - 1)]
+        return pltpu.make_async_remote_copy(
+            src_ref=box,
+            dst_ref=box,
+            send_sem=packet_ssem.at[to],
+            recv_sem=packet_rsem.at[to],
+            device_id={"sec": lax.rem(sec + 1, nsec)},
+            device_id_type=MESH,
+        )
+
+    visit(True, packet_to)
+    for side in (0, 1):
+        pl.when(near & sides[side][2])(functools.partial(packet_to, 2 * side, sec, ax + 2 * side - 1))
 
     sec_send[0] = first
     sec_send[1] = last
@@ -250,12 +351,10 @@
             dst_ref=sec_recv.at[1 - side],
             send_sem=sec_ssem.at[side],
             recv_sem=sec_rsem.at[1 - side],
-            device_id=others[-1] if side == 0 else others[0],
+            device_id=secs[side][1],
             device_id_type=MESH,
         )
 
-    sec_copy(0).start()
-    sec_copy(1).start()
 
     for k in range(fields):
         for p in range(planes):
@@ -274,53 +373,49 @@
         )
 
     for side in (0, 1):
-        pl.when(rads[side][0])(lambda side=side: rad_copy(side).start())
-
-    def ax_copy(side, c):
-        part = pl.ds(c * crow, crow)
-        return pltpu.make_async_remote_copy(
-            src_ref=state_ref.at[:, (planes - 1) if side == 1 else 0, part, :],
-            dst_ref=ghost.at[1 - side, :, part, :],
-            send_sem=ax_ssem.at[side, c],
-            recv_sem=ax_rsem.at[1 - side, c],
-            device_id=sides[side][1],
-            device_id_type=MESH,
-        )
-
-    for c in range(CHUNKS):
+        pl.when(secs[side][2])(lambda side=side: sec_copy(side).start())
+        pl.when(rads[side][2])(lambda side=side: rad_copy(side).start())
+    for side in (0, 1):
+        pl.when(secs[side][3])(lambda side=side: answered(sec_ready.at[side], sec_copy(side).start))
+    for side in (0, 1):
+        pl.when(sides[side][0] & (odd == side))(functools.partial(send_ax, side, tail))
+    for side in (0, 1):
+        pl.when(sides[side][3] & (odd != side) & ~sides[side][4])(
+            lambda side=side: answered(ax_ready.at[side], functools.partial(send_ax, side, range(CHUNKS)))
+        )
+
+    inv_r = inverse_radius(rows)
+    for p in range(planes):
+        for k in range(fields):
+            out_ref[k, p] = rhs(k, p, rows, inv_r)
+
+    for side in (0, 1):
+        pl.when(rads[side][3])(lambda side=side: answered(rad_ready.at[side], rad_copy(side).start))
+
+    @pl.when(near)
+    def _():
         for side in (0, 1):
-            pl.when(sides[side][0])(lambda side=side, c=c: ax_copy(side, c).start())
+            pl.when(sides[side][3] & ~sides[side][4])(functools.partial(packet_to, 2 * side, sec, ax + 2 * side - 1))
+        answers = sum(size(to, False) for to in range(3))
+        pl.when(answers > 0)(lambda: pl.semaphore_wait(packet_ready.at[0], answers))
+
+    visit(False, packet_to)
 
     sec_copy(1).wait_recv()
     sec_copy(0).wait_recv()
-    for side in (0, 1):
-        edge = 7 if side == 0 else rows + 8
-
-        @pl.when(rads[side][0])
-        def _():
-            rad_copy(1 - side).wait_recv()
-            for k in range(fields):
-                for p in range(planes):
-                    slot = k * planes + p
-                    rg[k, p, edge:edge + 1, :] = rad_recv[side, slot:slot + 1, :]
-
-    wide = lax.broadcasted_iota(jnp.int32, (rows, cells), 1)
     before = sec_recv[0]
     after = sec_recv[1]
-    inv_r = inverse_radius(rows)
+    thin = lax.broadcasted_iota(jnp.int32, (rows, 128), 1)
 
     def edges(packed, slot, to):
         column = [pltpu.roll(packed, (to - slot - t) % 128, 1) for t in range(tiles)]
-        column = jnp.concatenate(column, axis=0)
-        return jnp.concatenate([column, column], axis=1)
+        return jnp.concatenate(column, axis=0) * inv_r[:, :128]
 
     for p in range(planes):
         for k in range(fields):
-            h = hz[k, p]
             slot = (k * planes + p) * tiles
-            left = jnp.where(wide == 0, edges(before, slot, 0), pltpu.roll(h, 1, 1))
-            right = jnp.where(wide == cells - 1, edges(after, slot, 127), pltpu.roll(h, cells - 1, 1))
-            out_ref[k, p] = rhs(k, p, rows, left, right, inv_r)
+            out_ref[k, p, :, :128] += jnp.where(thin == 0, edges(before, slot, 0), 0.0)
+            out_ref[k, p, :, cells - 128:] -= jnp.where(thin == 127, edges(after, slot, 127), 0.0)
 
     def axial(c):
         for side in (0, 1):
@@ -335,6 +430,11 @@
                 for k, v in enumerate((s * mx, mx * hx + s * pr, mr * hx, mt * hx, (e + pr) * hx)):
                     out_ref[k, side, part, :] += v
 
+    @pl.when(sides[0][4])
+    def _():
+        answered(ax_ready.at[0], functools.partial(send_ax, 0, range(CHUNKS)))
+        packet_to(0, sec, ax - 1)
+
     axial(0)
 
     @pl.when(near)
@@ -343,6 +443,7 @@
         lane3 = lax.broadcasted_iota(jnp.int32, (planes, NEAR, 128), 2)
         fv3 = jnp.broadcast_to(fv[None], (planes, NEAR, 128))
         keeps = zero
+        scale = spread[2]
         for k in range(fields):
             for half in (0, 1):
                 x = out_ref[k, :, 0:NEAR, half * 128:(half + 1) * 128]
@@ -353,7 +454,7 @@
                 for n, d in enumerate(SHIFTS):
                     a = a + coef_f[n][None] * pltpu.roll(a, d, 2)
                     b = b + coef_b[n][None] * pltpu.roll(b, 128 - d, 2)
-                near_c[half, k] = a + b - x
+                near_c[half, k] = scale[None] * (a + b - x)
                 for p in range(planes):
                     for rt in (0, 1):
                         u = (k * planes + p) * 2 + rt
@@ -365,35 +466,25 @@
                             keeps = jnp.where(lane == npack + u, head, keeps)
         keep_ref[...] = keeps
 
+        @pl.when(reach)
+        def _():
+            pl.semaphore_wait(packet_ready.at[1], 1)
+            packet_to(jnp.where(ax == 0, 1, 0), 0, 0)
+
     for c in range(1, CHUNKS):
         axial(c)
 
     @pl.when(near)
     def _():
-        fv = factors()
-        packed = jnp.where(lane % 2 == 0, fv[0:8], fv[8:16])
-        rate = by_factor(packed, [math.exp(consts[f][1] * (128 // f)) for f in FACTORS])
-
-        def by_distance(m):
-            logs = [consts[f][1] * (cells // f) for f in FACTORS]
-            return by_factor(packed, [math.exp(g * (m - 1)) / -math.expm1(g * nsec) for g in logs])
-
-        ahead = [None] + [by_distance(m) for m in range(1, nsec + 1)]
-        back = [None] + [ahead[nsec - m] for m in range(1, nsec)] + [ahead[nsec]]
-        row = (lane % 2) * 8 + lax.broadcasted_iota(jnp.int32, (8, 128), 0)
-        edge = by_factor(packed, [1.0 / f for f in FACTORS]) / (row.astype(jnp.float32) + 0.5)
-        across = edge * by_factor(packed, [math.exp(consts[f][1] * (cells // f - 1)) for f in FACTORS])
         group = lane // npack
         sum_f, sum_b, sum_x = zero, zero, zero
-        packets(lambda to, k: packet_copy(2 - to, k).wait_recv())
-        for m in range(1, nsec + 1):
-            k = m % nsec
-            prev, after_m = (m - 1) or nsec, m % nsec + 1
-            own = inbox[1, k]
-            sum_f += own * jnp.where(group == 0, ahead[m], jnp.where(group == 2, across * ahead[prev], -edge * ahead[after_m]))
-            sum_b += own * jnp.where(group == 1, back[m], jnp.where(group == 2, edge * back[prev], -across * back[after_m]))
-            both = jnp.where(lane % 4 < 2, inbox[0, k], inbox[2, k])
-            sum_x += both * jnp.where(group == 4, ahead[m], back[m])
+        all_packets(1).wait_recv()
+        for side in (0, 1):
+            pl.when(sides[side][0])(all_packets(2 * side).wait_recv)
+        for m in range(nsec):
+            sum_f += inbox[1, m] * weights[0, m]
+            sum_b += inbox[1, m] * weights[1, m]
+            sum_x += jnp.where(lane % 4 < 2, inbox[0, m], inbox[2, m]) * weights[2, m]
 
         def down(v, groups):
             return pltpu.roll(v, 128 - groups * npack, 1)
@@ -401,14 +492,7 @@
         sum_f = sum_f + down(sum_f, 2) + down(sum_f, 3)
         sum_b = sum_b + down(sum_b, 1) + down(sum_b, 2)
         total_in = jnp.where(group == 0, sum_f, sum_b) + down(sum_x, 4)
-        inner = keep_ref[...] + rate * total_in
-        inv_f = by_factor(fv, [1.0 / f for f in FACTORS])
-        logs = by_factor(fv, [consts[f][1] for f in FACTORS])
-        scale = by_factor(fv, [consts[f][2] for f in FACTORS])
-        lane16 = lax.broadcasted_iota(jnp.int32, (NEAR, 128), 1).astype(jnp.float32)
-        block = jnp.floor(lane16 * inv_f)
-        grow = scale * jnp.exp(logs * (block + 1.0))
-        fall = scale * jnp.exp(logs * (128.0 * inv_f - block))
+        inner = keep_ref[...] + rate_ref[...] * total_in
         for k in range(fields):
             for p in range(planes):
                 for rt in (0, 1):
@@ -418,10 +502,25 @@
                         src_f, src_b = (total_in, inner) if half == 0 else (inner, total_in)
                         cf = jnp.broadcast_to(src_f[:, u:u + 1], (8, 128))
                         cb = jnp.broadcast_to(src_b[:, npack + u:npack + u + 1], (8, 128))
-                        w = scale[part] * near_c[half, k, p, part, :] + grow[part] * cf + fall[part] * cb
+                        w = near_c[half, k, p, part, :] + spread[0, part, :] * cf + spread[1, part, :] * cb
                         out_ref[k, p, part, half * 128:(half + 1) * 128] = w
 
-        packets(lambda to, k: packet_copy(to, k).wait_send())
+    for side in (0, 1):
+        @pl.when(rads[side][0])
+        def _():
+            rad_copy(1 - side).wait_recv()
+            row = 0 if side == 0 else rows - 1
+            sign = 1.0 if side == 0 else -1.0
+            for k in range(fields):
+                for p in range(planes):
+                    slot = k * planes + p
+                    out_ref[k, p, row:row + 1, :] += (sign * inv_r[row:row + 1, :]) * rad_recv[side, slot:slot + 1, :]
+
+    @pl.when(near)
+    def _():
+        all_packets(1).wait_send()
+        for side in (0, 1):
+            pl.when(sides[side][0])(all_packets(2 * side).wait_send)
 
     sec_copy(0).wait_send()
     sec_copy(1).wait_send()
@@ -441,11 +540,13 @@
         functools.partial(kernel, nsec, nrad, nax),
         out_shape=pltpu.VMEM(block, f32),
         in_specs=[
-            pl.BlockSpec(memory_space=pltpu.SMEM),
+            pl.BlockSpec(memory_space=pltpu.HBM),
             pl.BlockSpec(memory_space=pltpu.HBM),
         ],
         out_specs=pl.BlockSpec(memory_space=pltpu.VMEM),
         scratch_shapes=[
+            pltpu.SMEM((NEAR,), jnp.int32),
+            dma(()),
             pltpu.VMEM(block, f32),
             pltpu.VMEM(block, f32),
             pltpu.VMEM((fields, planes, rows + 16, cells), f32),
@@ -459,6 +560,9 @@
             pltpu.VMEM((len(SHIFTS), NEAR, 128), f32),
             pltpu.VMEM((NEAR, cells), f32),
             pltpu.VMEM((NEAR, cells), f32),
+            pltpu.VMEM((3, NEAR, 128), f32),
+            pltpu.VMEM((8, 128), f32),
+            pltpu.VMEM((3, nsec, 8, 128), f32),
             pltpu.VMEM((2, fields, planes, NEAR, 128), f32),
             pltpu.VMEM((8, 128), f32),
             pltpu.VMEM((8, 128), f32),
@@ -470,8 +574,12 @@
             dma((2,)),
             dma((2,)),
             dma((2,)),
-            dma((3, nsec)),
-            dma((3, nsec)),
+            dma((3,)),
+            dma((3,)),
+            pltpu.SemaphoreType.REGULAR((2,)),
+            pltpu.SemaphoreType.REGULAR((2,)),
+            pltpu.SemaphoreType.REGULAR((2,)),
+            pltpu.SemaphoreType.REGULAR((2,)),
         ],
         compiler_params=pltpu.CompilerParams(
             collective_id=0, has_side_effects=True, vmem_limit_bytes=32 * 1024 * 1024

time: 18.1 us -> 16.9 us (0.934)
  Pallas kernels: 17.1 us -> 16 us
    pallas_call x1, Pallas kernels: 17.1 us -> 16 us  [body(): pl.pallas_call(functools.partial(kernel, nsec, nrad, nax), out_shape=pltp...]
where the time goes in v3:
time: 16.9 us; the launch traced here: 16.8 us
  Pallas kernels  16 us (95%)
  local copies, waits for them, and re-layouts  0.84 us (5%)
    pallas_call x1, Pallas kernels, body(): pl.pallas_call(functools.partial(kernel, nsec, nrad, nax), out_shape=pltp...  16 us
    unnamed x1, local copies, waits for them, and re-layouts  0.84 us

profile of v3, /device:TPU:1, one launch (start us, length us, event | category | flops | bytes accessed | tf_op | source)
XLA Modules:
  0.0 16.8 jit_solution(344771182651642315)
XLA Ops:
  0.0 16.0 %shard_map.28 = f32[5,2,64,256]{3,2,1,0:T(8,128)S(1)} custom-call(s32[16]{0:T(128)} %coarsen_hbm.1, f32[5,2,64,256]{3,2,1,0:T(8,128)} %state_ref.1), custom_call_target="tpu_custom_call" | custom-call | flops 4000000 | bytes 2000000 | tf_op jit(solution)/shard_map/pallas_call | solution.py:539
  16.0 0.8 %copy.4 = f32[5,2,64,256]{3,2,1,0:T(8,128)} copy(f32[5,2,64,256]{3,2,1,0:T(8,128)S(1)} %shard_map.28) | data formatting | bytes 1310720

commit v4 on v3

--- a/solution.py
+++ b/solution.py
@@ -91,13 +91,13 @@
         (rad < nrad - 1, {"rad": rad + 1}, slow(sec, rad, ax), (rad < nrad - 1) & ~slow(sec, rad, ax)),
     ]
     secs = [
-        (True, {"sec": s}, rank(s, ax) < mine, rank(s, ax) > mine)
+        (True, {"sec": s}, rank(s, ax) < mine, rank(s, ax) > mine, slow(s, rad, ax))
         for s in (lax.rem(sec + nsec - 1, nsec), lax.rem(sec + 1, nsec))
     ]
     far = ~near
     for _, where, _, later, *_ in rads + sides:
         pl.when(later)(functools.partial(signal, barrier, where))
-    for _, where, _, later in secs:
+    for _, where, _, later, _ in secs:
         pl.when(far & later)(functools.partial(signal, barrier, where))
 
     tardy = slow(sec, rad, ax)
@@ -162,14 +162,13 @@
         for c in chunks:
             ax_copy(side, c).start()
 
-    head, tail = range(4), range(4, CHUNKS)
     odd = ax % 2
     for side in (0, 1):
         pl.when(sides[side][2] & (odd != side))(functools.partial(send_ax, side, range(CHUNKS)))
-        pl.when(sides[side][2] & (odd == side))(functools.partial(send_ax, side, head))
+        pl.when(sides[side][2] & (odd == side))(functools.partial(send_ax, side, range(CHUNKS)))
     for side in (0, 1):
         pl.when(sides[side][3] & (odd == side))(
-            lambda side=side: answered(ax_ready.at[side], functools.partial(send_ax, side, head))
+            lambda side=side: answered(ax_ready.at[side], functools.partial(send_ax, side, range(CHUNKS)))
         )
 
     lane = lax.broadcasted_iota(jnp.int32, (8, 128), 1)
@@ -216,11 +215,18 @@
         edge = by_factor(packed, [1.0 / f for f in FACTORS]) / (row.astype(jnp.float32) + 0.5)
         across = edge * by_factor(packed, [math.exp(consts[f][1] * (cells // f - 1)) for f in FACTORS])
         group = lane // (fields * planes * 2)
+        direct = edge * by_factor(packed, [math.exp(-consts[f][1]) for f in FACTORS])
         for m in range(1, nsec + 1):
             prev, after_m = (m - 1) or nsec, m % nsec + 1
             k = m % nsec
-            weights[0, k] = jnp.where(group == 0, ahead[m], jnp.where(group == 2, across * ahead[prev], -edge * ahead[after_m]))
-            weights[1, k] = jnp.where(group == 1, back[m], jnp.where(group == 2, edge * back[prev], -across * back[after_m]))
+            from_last, from_first = across * ahead[prev], -edge * ahead[after_m]
+            to_last, to_first = edge * back[prev], -across * back[after_m]
+            if m == 1:
+                from_last = from_last + direct
+            if m == nsec - 1:
+                to_first = to_first - direct
+            weights[0, k] = jnp.where(group == 0, ahead[m], jnp.where(group == 2, from_last, from_first))
+            weights[1, k] = jnp.where(group == 1, back[m], jnp.where(group == 2, to_last, to_first))
             weights[2, k] = jnp.where(group == 4, ahead[m], back[m])
         for side in (0, 1):
             @pl.when(jnp.logical_not(sides[side][0]))
@@ -286,31 +292,78 @@
         place = rad * rows + lax.broadcasted_iota(jnp.int32, (size, cells), 0)
         return 1.0 / (place.astype(jnp.float32) + 0.5)
 
+    sec_send[0] = first
+    sec_send[1] = last
+
+    def sec_copy(side):
+        return pltpu.make_async_remote_copy(
+            src_ref=sec_send.at[side],
+            dst_ref=sec_recv.at[1 - side],
+            send_sem=sec_ssem.at[side],
+            recv_sem=sec_rsem.at[1 - side],
+            device_id=secs[side][1],
+            device_id_type=MESH,
+        )
+
+
+    for k in range(fields):
+        for p in range(planes):
+            slot = k * planes + p
+            rad_send[0, slot:slot + 1, :] = rg[k, p, 8:9, :]
+            rad_send[1, slot:slot + 1, :] = rg[k, p, rows + 7:rows + 8, :]
+
+    def rad_copy(side):
+        return pltpu.make_async_remote_copy(
+            src_ref=rad_send.at[side],
+            dst_ref=rad_recv.at[1 - side],
+            send_sem=rad_ssem.at[side],
+            recv_sem=rad_rsem.at[1 - side],
+            device_id=rads[side][1],
+            device_id_type=MESH,
+        )
+
+    for side in (0, 1):
+        pl.when(secs[side][2])(lambda side=side: sec_copy(side).start())
+        pl.when(rads[side][2])(lambda side=side: rad_copy(side).start())
     @pl.when(near)
     def _():
         inv_r = inverse_radius(NEAR)
         wf, wb = weigh_f[...], weigh_b[...]
         pack = zero
-
-        def put(pack, group, u, column):
-            return jnp.where(lane == group * npack + u, jnp.broadcast_to(column, (8, 128)), pack)
-
-        def total(v):
-            return jnp.sum(v[:, :128] + v[:, 128:], axis=1, keepdims=True)
+        terms = {}
+
+        def halves(v):
+            return v[:, :128] + v[:, 128:]
 
         for k in range(fields):
             for p in range(planes):
                 h = hz[k, p, 0:NEAR, :]
                 v = rhs(k, p, NEAR, inv_r)
                 beside = fx[k, 1, 0:NEAR, :] if p == 0 else -fx[k, 0, 0:NEAR, :]
-                columns = (
-                    total(v * wf), total(v * wb), h[:, cells - 1:], h[:, :1],
-                    total(beside * wf), total(beside * wb),
-                )
+                sums = {0: halves(v * wf), 1: halves(v * wb), 4: halves(beside * wf), 5: halves(beside * wb)}
                 for rt in (0, 1):
                     u = (k * planes + p) * 2 + rt
-                    for group, column in enumerate(columns):
-                        pack = put(pack, group, u, column[rt * 8:rt * 8 + 8])
+                    part = slice(rt * 8, rt * 8 + 8)
+                    for group, v_sum in sums.items():
+                        terms[group * npack + u] = v_sum[part]
+                    at = 2 * npack + u
+                    pack = jnp.where(lane == at, pltpu.roll(h[part, cells - 128:], at + 1, 1), pack)
+                    at = 3 * npack + u
+                    pack = jnp.where(lane == at, pltpu.roll(h[part, :128], at, 1), pack)
+        width = 1
+        while width < 128:
+            high = (lane & width) != 0
+            merged = {}
+            for i in range(64 // width):
+                x, y = terms.get(2 * i), terms.get(2 * i + 1)
+                if x is not None and y is not None:
+                    merged[i] = jnp.where(high, y, x) + pltpu.roll(jnp.where(high, x, y), width, 1)
+                elif x is not None or y is not None:
+                    x = y if x is None else x
+                    merged[i] = x + pltpu.roll(x, width, 1)
+            terms, width = merged, width * 2
+        middle = (lane >= 2 * npack) & (lane < 4 * npack)
+        pack = jnp.where(middle, pack, terms[0])
         packet[...] = pack
         inbox[1, 0] = pack
 
@@ -342,55 +395,19 @@
     for side in (0, 1):
         pl.when(near & sides[side][2])(functools.partial(packet_to, 2 * side, sec, ax + 2 * side - 1))
 
-    sec_send[0] = first
-    sec_send[1] = last
-
-    def sec_copy(side):
-        return pltpu.make_async_remote_copy(
-            src_ref=sec_send.at[side],
-            dst_ref=sec_recv.at[1 - side],
-            send_sem=sec_ssem.at[side],
-            recv_sem=sec_rsem.at[1 - side],
-            device_id=secs[side][1],
-            device_id_type=MESH,
-        )
-
-
-    for k in range(fields):
-        for p in range(planes):
-            slot = k * planes + p
-            rad_send[0, slot:slot + 1, :] = rg[k, p, 8:9, :]
-            rad_send[1, slot:slot + 1, :] = rg[k, p, rows + 7:rows + 8, :]
-
-    def rad_copy(side):
-        return pltpu.make_async_remote_copy(
-            src_ref=rad_send.at[side],
-            dst_ref=rad_recv.at[1 - side],
-            send_sem=rad_ssem.at[side],
-            recv_sem=rad_rsem.at[1 - side],
-            device_id=rads[side][1],
-            device_id_type=MESH,
-        )
-
-    for side in (0, 1):
-        pl.when(secs[side][2])(lambda side=side: sec_copy(side).start())
-        pl.when(rads[side][2])(lambda side=side: rad_copy(side).start())
-    for side in (0, 1):
-        pl.when(secs[side][3])(lambda side=side: answered(sec_ready.at[side], sec_copy(side).start))
-    for side in (0, 1):
-        pl.when(sides[side][0] & (odd == side))(functools.partial(send_ax, side, tail))
     for side in (0, 1):
         pl.when(sides[side][3] & (odd != side) & ~sides[side][4])(
             lambda side=side: answered(ax_ready.at[side], functools.partial(send_ax, side, range(CHUNKS)))
         )
+    for side in (0, 1):
+        pl.when(secs[side][3] & ~secs[side][4])(lambda side=side: answered(sec_ready.at[side], sec_copy(side).start))
 
     inv_r = inverse_radius(rows)
     for p in range(planes):
         for k in range(fields):
             out_ref[k, p] = rhs(k, p, rows, inv_r)
 
-    for side in (0, 1):
-        pl.when(rads[side][3])(lambda side=side: answered(rad_ready.at[side], rad_copy(side).start))
+    pl.when(rads[1][3])(lambda: answered(rad_ready.at[1], rad_copy(1).start))
 
     @pl.when(near)
     def _():
@@ -401,21 +418,18 @@
 
     visit(False, packet_to)
 
-    sec_copy(1).wait_recv()
-    sec_copy(0).wait_recv()
-    before = sec_recv[0]
-    after = sec_recv[1]
-    thin = lax.broadcasted_iota(jnp.int32, (rows, 128), 1)
-
-    def edges(packed, slot, to):
-        column = [pltpu.roll(packed, (to - slot - t) % 128, 1) for t in range(tiles)]
-        return jnp.concatenate(column, axis=0) * inv_r[:, :128]
-
-    for p in range(planes):
-        for k in range(fields):
-            slot = (k * planes + p) * tiles
-            out_ref[k, p, :, :128] += jnp.where(thin == 0, edges(before, slot, 0), 0.0)
-            out_ref[k, p, :, cells - 128:] -= jnp.where(thin == 127, edges(after, slot, 127), 0.0)
+    @pl.when(sides[0][4])
+    def _():
+        answered(ax_ready.at[0], functools.partial(send_ax, 0, range(CHUNKS)))
+        packet_to(0, sec, ax - 1)
+
+    @pl.when(reach)
+    def _():
+        pl.semaphore_wait(packet_ready.at[1], 1)
+        packet_to(jnp.where(ax == 0, 1, 0), 0, 0)
+
+    for side in (0, 1):
+        pl.when(secs[side][4])(lambda side=side: answered(sec_ready.at[side], sec_copy(side).start))
 
     def axial(c):
         for side in (0, 1):
@@ -429,11 +443,6 @@
                 hx = s * ux
                 for k, v in enumerate((s * mx, mx * hx + s * pr, mr * hx, mt * hx, (e + pr) * hx)):
                     out_ref[k, side, part, :] += v
-
-    @pl.when(sides[0][4])
-    def _():
-        answered(ax_ready.at[0], functools.partial(send_ax, 0, range(CHUNKS)))
-        packet_to(0, sec, ax - 1)
 
     axial(0)
 
@@ -466,10 +475,21 @@
                             keeps = jnp.where(lane == npack + u, head, keeps)
         keep_ref[...] = keeps
 
-        @pl.when(reach)
-        def _():
-            pl.semaphore_wait(packet_ready.at[1], 1)
-            packet_to(jnp.where(ax == 0, 1, 0), 0, 0)
+    sec_copy(1).wait_recv()
+    sec_copy(0).wait_recv()
+    before = sec_recv[0]
+    after = sec_recv[1]
+    thin = lax.broadcasted_iota(jnp.int32, (rows, 128), 1)
+
+    def edges(packed, slot, to):
+        column = [pltpu.roll(packed, (to - slot - t) % 128, 1) for t in range(tiles)]
+        return jnp.concatenate(column, axis=0) * inv_r[:, :128]
+
+    for p in range(planes):
+        for k in range(fields):
+            slot = (k * planes + p) * tiles
+            out_ref[k, p, :, :128] += jnp.where(thin == 0, edges(before, slot, 0), 0.0)
+            out_ref[k, p, :, cells - 128:] -= jnp.where(thin == 127, edges(after, slot, 127), 0.0)
 
     for c in range(1, CHUNKS):
         axial(c)
@@ -505,6 +525,7 @@
                         w = near_c[half, k, p, part, :] + spread[0, part, :] * cf + spread[1, part, :] * cb
                         out_ref[k, p, part, half * 128:(half + 1) * 128] = w
 
+    pl.when(rads[0][3])(lambda: answered(rad_ready.at[0], rad_copy(0).start))
     for side in (0, 1):
         @pl.when(rads[side][0])
         def _():

time: 16.9 us -> 14.7 us (0.87)
  Pallas kernels: 16 us -> 13.7 us
    pallas_call x1, Pallas kernels: 16 us -> 13.7 us  [body(): pl.pallas_call(functools.partial(kernel, nsec, nrad, nax), out_shape=pltp...]
where the time goes in v4:
time: 14.7 us; the launch traced here: 14.5 us
  Pallas kernels  13.7 us (93%)
  local copies, waits for them, and re-layouts  0.84 us (6%)
    pallas_call x1, Pallas kernels, body(): pl.pallas_call(functools.partial(kernel, nsec, nrad, nax), out_shape=pltp...  13.7 us
    unnamed x1, local copies, waits for them, and re-layouts  0.84 us

profile of v4, /device:TPU:1, one launch (start us, length us, event | category | flops | bytes accessed | tf_op | source)
XLA Modules:
  0.0 14.5 jit_solution(10977557173160566342)
XLA Ops:
  0.0 13.7 %shard_map.28 = f32[5,2,64,256]{3,2,1,0:T(8,128)S(1)} custom-call(s32[16]{0:T(128)} %coarsen_hbm.1, f32[5,2,64,256]{3,2,1,0:T(8,128)} %state_ref.1), custom_call_target="tpu_custom_call" | custom-call | flops 4000000 | bytes 2000000 | tf_op jit(solution)/shard_map/pallas_call | solution.py:560
  13.7 0.8 %copy.4 = f32[5,2,64,256]{3,2,1,0:T(8,128)} copy(f32[5,2,64,256]{3,2,1,0:T(8,128)S(1)} %shard_map.28) | data formatting | bytes 1310720

commit v5 on v4

--- a/solution.py
+++ b/solution.py
@@ -129,47 +129,6 @@
 
     visit(False, lambda to, s, a: signal(barrier, {"sec": s, "ax": a}))
     pl.when(reach)(lambda: signal(barrier, {"sec": 0, "ax": 0}))
-
-    def number(flags):
-        return sum(jnp.where(flag, 1, 0) for flag in flags)
-
-    count = number(v[2] for v in rads + sides)
-    count = count + jnp.where(near, sum(size(to, True) for to in range(3)), number(v[2] for v in secs))
-    pl.when(count > 0)(lambda: pl.semaphore_wait(barrier, count))
-
-    for ready, pairs in ((ax_ready, sides), (sec_ready, secs), (rad_ready, rads)):
-        for side in (0, 1):
-            pl.when(pairs[side][2])(functools.partial(signal, ready.at[1 - side], pairs[side][1]))
-
-    visit(True, lambda to, s, a: signal(packet_ready.at[jnp.where(tardy, 1, 0)], {"sec": s, "ax": a}))
-
-    def ax_copy(side, c):
-        part = pl.ds(c * crow, crow)
-        return pltpu.make_async_remote_copy(
-            src_ref=state_ref.at[:, (planes - 1) if side == 1 else 0, part, :],
-            dst_ref=ghost.at[1 - side, :, part, :],
-            send_sem=ax_ssem.at[side, c],
-            recv_sem=ax_rsem.at[1 - side, c],
-            device_id=sides[side][1],
-            device_id_type=MESH,
-        )
-
-    def answered(ready, send):
-        pl.semaphore_wait(ready, 1)
-        send()
-
-    def send_ax(side, chunks):
-        for c in chunks:
-            ax_copy(side, c).start()
-
-    odd = ax % 2
-    for side in (0, 1):
-        pl.when(sides[side][2] & (odd != side))(functools.partial(send_ax, side, range(CHUNKS)))
-        pl.when(sides[side][2] & (odd == side))(functools.partial(send_ax, side, range(CHUNKS)))
-    for side in (0, 1):
-        pl.when(sides[side][3] & (odd == side))(
-            lambda side=side: answered(ax_ready.at[side], functools.partial(send_ax, side, range(CHUNKS)))
-        )
 
     lane = lax.broadcasted_iota(jnp.int32, (8, 128), 1)
     consts = filter_constants(total)
@@ -238,7 +197,7 @@
             for edge in (7, rows + 8):
                 rg[k, p, edge:edge + 1, :] = jnp.zeros((1, cells), jnp.float32)
 
-    for copy in loads:
+    for copy in loads[:2]:
         copy.wait()
 
     row8 = lax.broadcasted_iota(jnp.int32, (8, cells), 0)
@@ -272,7 +231,7 @@
         return first, last
 
     zero = jnp.zeros((8, 128), jnp.float32)
-    first, last = lax.fori_loop(0, tiles, fluxes, (zero, zero))
+    first, last = lax.fori_loop(0, NEAR // 8 + 1, fluxes, (zero, zero))
     npack = fields * planes * 2
 
     def rhs(k, p, size, inv_r):
@@ -292,39 +251,42 @@
         place = rad * rows + lax.broadcasted_iota(jnp.int32, (size, cells), 0)
         return 1.0 / (place.astype(jnp.float32) + 0.5)
 
-    sec_send[0] = first
-    sec_send[1] = last
-
-    def sec_copy(side):
+    def number(flags):
+        return sum(jnp.where(flag, 1, 0) for flag in flags)
+
+    count = number(v[2] for v in rads + sides)
+    count = count + jnp.where(near, sum(size(to, True) for to in range(3)), number(v[2] for v in secs))
+    pl.when(count > 0)(lambda: pl.semaphore_wait(barrier, count))
+
+    for ready, pairs in ((ax_ready, sides), (sec_ready, secs), (rad_ready, rads)):
+        for side in (0, 1):
+            pl.when(pairs[side][2])(functools.partial(signal, ready.at[1 - side], pairs[side][1]))
+
+    def ax_copy(side, c):
+        part = pl.ds(c * crow, crow)
         return pltpu.make_async_remote_copy(
-            src_ref=sec_send.at[side],
-            dst_ref=sec_recv.at[1 - side],
-            send_sem=sec_ssem.at[side],
-            recv_sem=sec_rsem.at[1 - side],
-            device_id=secs[side][1],
+            src_ref=state_ref.at[:, (planes - 1) if side == 1 else 0, part, :],
+            dst_ref=ghost.at[1 - side, :, part, :],
+            send_sem=ax_ssem.at[side, c],
+            recv_sem=ax_rsem.at[1 - side, c],
+            device_id=sides[side][1],
             device_id_type=MESH,
         )
 
-
-    for k in range(fields):
-        for p in range(planes):
-            slot = k * planes + p
-            rad_send[0, slot:slot + 1, :] = rg[k, p, 8:9, :]
-            rad_send[1, slot:slot + 1, :] = rg[k, p, rows + 7:rows + 8, :]
-
-    def rad_copy(side):
-        return pltpu.make_async_remote_copy(
-            src_ref=rad_send.at[side],
-            dst_ref=rad_recv.at[1 - side],
-            send_sem=rad_ssem.at[side],
-            recv_sem=rad_rsem.at[1 - side],
-            device_id=rads[side][1],
-            device_id_type=MESH,
-        )
-
-    for side in (0, 1):
-        pl.when(secs[side][2])(lambda side=side: sec_copy(side).start())
-        pl.when(rads[side][2])(lambda side=side: rad_copy(side).start())
+    def answered(ready, send):
+        pl.semaphore_wait(ready, 1)
+        send()
+
+    def send_ax(side, chunks):
+        for c in chunks:
+            ax_copy(side, c).start()
+
+    odd = ax % 2
+    for side in (0, 1):
+        pl.when(sides[side][2] & (odd != side))(functools.partial(send_ax, side, range(CHUNKS)))
+    visit(True, lambda to, s, a: signal(packet_ready.at[jnp.where(tardy, 1, 0)], {"sec": s, "ax": a}))
+    for side in (0, 1):
+        pl.when(sides[side][2] & (odd == side))(functools.partial(send_ax, side, range(CHUNKS)))
     @pl.when(near)
     def _():
         inv_r = inverse_radius(NEAR)
@@ -391,10 +353,50 @@
             device_id_type=MESH,
         )
 
+    for side in (0, 1):
+        pl.when(near & sides[side][2])(functools.partial(packet_to, 2 * side, sec, ax + 2 * side - 1))
     visit(True, packet_to)
-    for side in (0, 1):
-        pl.when(near & sides[side][2])(functools.partial(packet_to, 2 * side, sec, ax + 2 * side - 1))
-
+
+    for copy in loads[2:]:
+        copy.wait()
+    first, last = lax.fori_loop(NEAR // 8 + 1, tiles, fluxes, (first, last))
+    sec_send[0] = first
+    sec_send[1] = last
+
+    def sec_copy(side):
+        return pltpu.make_async_remote_copy(
+            src_ref=sec_send.at[side],
+            dst_ref=sec_recv.at[1 - side],
+            send_sem=sec_ssem.at[side],
+            recv_sem=sec_rsem.at[1 - side],
+            device_id=secs[side][1],
+            device_id_type=MESH,
+        )
+
+
+    for k in range(fields):
+        for p in range(planes):
+            slot = k * planes + p
+            rad_send[0, slot:slot + 1, :] = rg[k, p, 8:9, :]
+            rad_send[1, slot:slot + 1, :] = rg[k, p, rows + 7:rows + 8, :]
+
+    def rad_copy(side):
+        return pltpu.make_async_remote_copy(
+            src_ref=rad_send.at[side],
+            dst_ref=rad_recv.at[1 - side],
+            send_sem=rad_ssem.at[side],
+            recv_sem=rad_rsem.at[1 - side],
+            device_id=rads[side][1],
+            device_id_type=MESH,
+        )
+
+    for side in (0, 1):
+        pl.when(secs[side][2])(lambda side=side: sec_copy(side).start())
+        pl.when(rads[side][2])(lambda side=side: rad_copy(side).start())
+    for side in (0, 1):
+        pl.when(sides[side][3] & (odd == side))(
+            lambda side=side: answered(ax_ready.at[side], functools.partial(send_ax, side, range(CHUNKS)))
+        )
     for side in (0, 1):
         pl.when(sides[side][3] & (odd != side) & ~sides[side][4])(
             lambda side=side: answered(ax_ready.at[side], functools.partial(send_ax, side, range(CHUNKS)))
@@ -418,21 +420,8 @@
 
     visit(False, packet_to)
 
-    @pl.when(sides[0][4])
-    def _():
-        answered(ax_ready.at[0], functools.partial(send_ax, 0, range(CHUNKS)))
-        packet_to(0, sec, ax - 1)
-
-    @pl.when(reach)
-    def _():
-        pl.semaphore_wait(packet_ready.at[1], 1)
-        packet_to(jnp.where(ax == 0, 1, 0), 0, 0)
-
-    for side in (0, 1):
-        pl.when(secs[side][4])(lambda side=side: answered(sec_ready.at[side], sec_copy(side).start))
-
-    def axial(c):
-        for side in (0, 1):
+    def axial(c, both=(0, 1)):
+        for side in both:
             @pl.when(sides[side][0])
             def _():
                 ax_copy(1 - side, c).wait_recv()
@@ -444,36 +433,50 @@
                 for k, v in enumerate((s * mx, mx * hx + s * pr, mr * hx, mt * hx, (e + pr) * hx)):
                     out_ref[k, side, part, :] += v
 
-    axial(0)
-
-    @pl.when(near)
-    def _():
+    def scan(p):
         fv = factors()
-        lane3 = lax.broadcasted_iota(jnp.int32, (planes, NEAR, 128), 2)
-        fv3 = jnp.broadcast_to(fv[None], (planes, NEAR, 128))
+        lane16 = lax.broadcasted_iota(jnp.int32, (NEAR, 128), 1)
         keeps = zero
         scale = spread[2]
         for k in range(fields):
             for half in (0, 1):
-                x = out_ref[k, :, 0:NEAR, half * 128:(half + 1) * 128]
+                x = out_ref[k, p, 0:NEAR, half * 128:(half + 1) * 128]
                 for d in (1, 2, 4, 8):
-                    swap = jnp.where((lane3 & d) == 0, pltpu.roll(x, 128 - d, 2), pltpu.roll(x, d, 2))
-                    x = jnp.where(fv3 > d, 0.5 * (x + swap), x)
+                    swap = jnp.where((lane16 & d) == 0, pltpu.roll(x, 128 - d, 1), pltpu.roll(x, d, 1))
+                    x = jnp.where(fv > d, 0.5 * (x + swap), x)
                 a, b = x, x
                 for n, d in enumerate(SHIFTS):
-                    a = a + coef_f[n][None] * pltpu.roll(a, d, 2)
-                    b = b + coef_b[n][None] * pltpu.roll(b, 128 - d, 2)
-                near_c[half, k] = scale[None] * (a + b - x)
-                for p in range(planes):
-                    for rt in (0, 1):
-                        u = (k * planes + p) * 2 + rt
-                        if half == 0:
-                            tail = pltpu.roll(a[p, rt * 8:rt * 8 + 8, :], (u + 1) % 128, 1)
-                            keeps = jnp.where(lane == u, tail, keeps)
-                        else:
-                            head = pltpu.roll(b[p, rt * 8:rt * 8 + 8, :], npack + u, 1)
-                            keeps = jnp.where(lane == npack + u, head, keeps)
-        keep_ref[...] = keeps
+                    a = a + coef_f[n] * pltpu.roll(a, d, 1)
+                    b = b + coef_b[n] * pltpu.roll(b, 128 - d, 1)
+                near_c[half, k, p] = scale * (a + b - x)
+                for rt in (0, 1):
+                    u = (k * planes + p) * 2 + rt
+                    if half == 0:
+                        tail = pltpu.roll(a[rt * 8:rt * 8 + 8], (u + 1) % 128, 1)
+                        keeps = jnp.where(lane == u, tail, keeps)
+                    else:
+                        head = pltpu.roll(b[rt * 8:rt * 8 + 8], npack + u, 1)
+                        keeps = jnp.where(lane == npack + u, head, keeps)
+        keep_ref[...] = keeps if p == planes - 1 else keep_ref[...] + keeps
+
+    axial(0, (1,))
+    pl.when(near)(functools.partial(scan, 1))
+
+    @pl.when(sides[0][4])
+    def _():
+        answered(ax_ready.at[0], functools.partial(send_ax, 0, range(CHUNKS)))
+        packet_to(0, sec, ax - 1)
+
+    @pl.when(reach)
+    def _():
+        pl.semaphore_wait(packet_ready.at[1], 1)
+        packet_to(jnp.where(ax == 0, 1, 0), 0, 0)
+
+    for side in (0, 1):
+        pl.when(secs[side][4])(lambda side=side: answered(sec_ready.at[side], sec_copy(side).start))
+
+    axial(0, (0,))
+    pl.when(near)(functools.partial(scan, 0))
 
     sec_copy(1).wait_recv()
     sec_copy(0).wait_recv()

time: 14.7 us -> 14.5 us (0.986)
  the two profiles are of different devices: /device:TPU:1 before, /device:TPU:57 now
where the time goes in v5:
time: 14.5 us; the launch traced here: 14.3 us
  Pallas kernels  13.5 us (93%)
  local copies, waits for them, and re-layouts  0.84 us (6%)
    pallas_call x1, Pallas kernels, body(): pl.pallas_call(functools.partial(kernel, nsec, nrad, nax), out_shape=pltp...  13.5 us
    unnamed x1, local copies, waits for them, and re-layouts  0.84 us

profile of v5, /device:TPU:57, one launch (start us, length us, event | category | flops | bytes accessed | tf_op | source)
XLA Modules:
  0.0 14.3 jit_solution(6252461430973127433)
XLA Ops:
  0.0 13.5 %shard_map.28 = f32[5,2,64,256]{3,2,1,0:T(8,128)S(1)} custom-call(s32[16]{0:T(128)} %coarsen_hbm.1, f32[5,2,64,256]{3,2,1,0:T(8,128)} %state_ref.1), custom_call_target="tpu_custom_call" | custom-call | flops 4000000 | bytes 2000000 | tf_op jit(solution)/shard_map/pallas_call | solution.py:563
  13.5 0.8 %copy.4 = f32[5,2,64,256]{3,2,1,0:T(8,128)} copy(f32[5,2,64,256]{3,2,1,0:T(8,128)S(1)} %shard_map.28) | data formatting | bytes 1310720

commit v6 on v5

--- a/solution.py
+++ b/solution.py
@@ -104,19 +104,28 @@
     turn = jnp.where(sec < nsec // 2, sec, nsec + nsec // 2 - 1 - sec)
     reach = near & (ax <= 1) & (sec != 0)
 
-    def span(to, earlier):
-        if not earlier:
-            return jnp.where(tardy, nsec, turn + 1), nsec
-        return jnp.where(tardy | (ax + to == 1), 1, 0), jnp.where(tardy, nsec, turn)
+    middle = turn == 3
+    after = (turn >= 4) & (turn < 7)
+
+    def spans(to, kind):
+        first = jnp.where(tardy | (ax + to == 1), 1, 0)
+        upto = jnp.where(tardy, nsec, turn)
+        beyond = jnp.where(tardy, nsec, turn + 1)
+        if kind == "greet":
+            return (beyond, nsec), (jnp.where(after, 3, 0), jnp.where(after, 4, 0))
+        if kind == "answer":
+            return (first, jnp.where(after, 3, upto)), (jnp.where(after, 4, 0), jnp.where(after, turn, 0))
+        if kind == "early":
+            return (first, upto), (jnp.where(middle, 4, 0), jnp.where(middle, 7, 0))
+        return (beyond, jnp.where(middle, 4, nsec)), (jnp.where(middle, 7, 0), jnp.where(middle, nsec, 0))
 
     def there(to):
         return near if to == 1 else near & sides[to // 2][0]
 
-    def size(to, earlier):
-        lo, hi = span(to, earlier)
-        return jnp.where(there(to), jnp.maximum(hi - lo, 0), 0)
-
-    def visit(earlier, act):
+    def size(to, kind):
+        return jnp.where(there(to), sum(jnp.maximum(hi - lo, 0) for lo, hi in spans(to, kind)), 0)
+
+    def visit(kind, act):
         for to in (1, 0, 2):
             def step(t, carry):
                 s = jnp.where(t < nsec // 2, t, nsec + nsec // 2 - 1 - t)
@@ -125,9 +134,10 @@
 
             @pl.when(there(to))
             def _():
-                lax.fori_loop(*span(to, earlier), step, 0)
-
-    visit(False, lambda to, s, a: signal(barrier, {"sec": s, "ax": a}))
+                for lo, hi in spans(to, kind):
+                    lax.fori_loop(lo, hi, step, 0)
+
+    visit("greet", lambda to, s, a: signal(barrier, {"sec": s, "ax": a}))
     pl.when(reach)(lambda: signal(barrier, {"sec": 0, "ax": 0}))
 
     lane = lax.broadcasted_iota(jnp.int32, (8, 128), 1)
@@ -154,8 +164,15 @@
         logs = by_factor(fw, [consts[f][1] for f in FACTORS])
         block = lax.broadcasted_iota(jnp.int32, (NEAR, cells), 1).astype(jnp.float32)
         block = jnp.floor(block * share)
-        weigh_f[...] = share * jnp.exp(logs * (cells * share - 1.0 - block))
-        weigh_b[...] = share * jnp.exp(logs * block)
+        wide = lax.broadcasted_iota(jnp.int32, (NEAR, cells), 1)
+        inv_r = 1.0 / (lax.broadcasted_iota(jnp.int32, (NEAR, cells), 0).astype(jnp.float32) + 0.5)
+        for ref, power in ((weigh_f, cells * share - 1.0 - block), (weigh_b, block)):
+            w = share * jnp.exp(logs * power)
+            ref[0] = w
+            ref[1] = w * inv_r
+            ref[2] = inv_r * (
+                jnp.where(wide == cells - 1, 0.0, pltpu.roll(w, cells - 1, 1)) - jnp.where(wide == 0, 0.0, pltpu.roll(w, 1, 1))
+            )
         scale = by_factor(fv, [consts[f][2] for f in FACTORS])
         share, logs, block = share[:, :128], logs[:, :128], block[:, :128]
         spread[0] = scale * jnp.exp(logs * (block + 1.0))
@@ -255,7 +272,7 @@
         return sum(jnp.where(flag, 1, 0) for flag in flags)
 
     count = number(v[2] for v in rads + sides)
-    count = count + jnp.where(near, sum(size(to, True) for to in range(3)), number(v[2] for v in secs))
+    count = count + jnp.where(near, sum(size(to, "early") for to in range(3)), number(v[2] for v in secs))
     pl.when(count > 0)(lambda: pl.semaphore_wait(barrier, count))
 
     for ready, pairs in ((ax_ready, sides), (sec_ready, secs), (rad_ready, rads)):
@@ -284,13 +301,11 @@
     odd = ax % 2
     for side in (0, 1):
         pl.when(sides[side][2] & (odd != side))(functools.partial(send_ax, side, range(CHUNKS)))
-    visit(True, lambda to, s, a: signal(packet_ready.at[jnp.where(tardy, 1, 0)], {"sec": s, "ax": a}))
+    visit("answer", lambda to, s, a: signal(packet_ready.at[jnp.where(tardy, 1, 0)], {"sec": s, "ax": a}))
     for side in (0, 1):
         pl.when(sides[side][2] & (odd == side))(functools.partial(send_ax, side, range(CHUNKS)))
     @pl.when(near)
     def _():
-        inv_r = inverse_radius(NEAR)
-        wf, wb = weigh_f[...], weigh_b[...]
         pack = zero
         terms = {}
 
@@ -300,9 +315,16 @@
         for k in range(fields):
             for p in range(planes):
                 h = hz[k, p, 0:NEAR, :]
-                v = rhs(k, p, NEAR, inv_r)
+                g = rg[k, p, 7:NEAR + 7, :] - rg[k, p, 9:NEAR + 9, :]
+                if k == 2:
+                    g = g + (2.0 * dtheta) * hz[3, p, 0:NEAR, :]
+                if k == 3:
+                    g = g - (2.0 * dtheta) * hz[2, p, 0:NEAR, :]
                 beside = fx[k, 1, 0:NEAR, :] if p == 0 else -fx[k, 0, 0:NEAR, :]
-                sums = {0: halves(v * wf), 1: halves(v * wb), 4: halves(beside * wf), 5: halves(beside * wb)}
+                sums = {}
+                for n, w in enumerate((weigh_f, weigh_b)):
+                    sums[4 + n] = halves(beside * w[0])
+                    sums[n] = halves(g * w[1] + h * w[2]) - sums[4 + n]
                 for rt in (0, 1):
                     u = (k * planes + p) * 2 + rt
                     part = slice(rt * 8, rt * 8 + 8)
@@ -355,7 +377,7 @@
 
     for side in (0, 1):
         pl.when(near & sides[side][2])(functools.partial(packet_to, 2 * side, sec, ax + 2 * side - 1))
-    visit(True, packet_to)
+    visit("early", packet_to)
 
     for copy in loads[2:]:
         copy.wait()
@@ -415,10 +437,10 @@
     def _():
         for side in (0, 1):
             pl.when(sides[side][3] & ~sides[side][4])(functools.partial(packet_to, 2 * side, sec, ax + 2 * side - 1))
-        answers = sum(size(to, False) for to in range(3))
+        answers = sum(size(to, "late") for to in range(3))
         pl.when(answers > 0)(lambda: pl.semaphore_wait(packet_ready.at[0], answers))
 
-    visit(False, packet_to)
+    visit("late", packet_to)
 
     def axial(c, both=(0, 1)):
         for side in both:
@@ -481,7 +503,7 @@
     sec_copy(1).wait_recv()
     sec_copy(0).wait_recv()
     before = sec_recv[0]
-    after = sec_recv[1]
+    behind = sec_recv[1]
     thin = lax.broadcasted_iota(jnp.int32, (rows, 128), 1)
 
     def edges(packed, slot, to):
@@ -492,10 +514,22 @@
         for k in range(fields):
             slot = (k * planes + p) * tiles
             out_ref[k, p, :, :128] += jnp.where(thin == 0, edges(before, slot, 0), 0.0)
-            out_ref[k, p, :, cells - 128:] -= jnp.where(thin == 127, edges(after, slot, 127), 0.0)
+            out_ref[k, p, :, cells - 128:] -= jnp.where(thin == 127, edges(behind, slot, 127), 0.0)
 
     for c in range(1, CHUNKS):
         axial(c)
+
+    pl.when(rads[0][3])(lambda: answered(rad_ready.at[0], rad_copy(0).start))
+    for side in (0, 1):
+        @pl.when(rads[side][0])
+        def _():
+            rad_copy(1 - side).wait_recv()
+            row = 0 if side == 0 else rows - 1
+            sign = 1.0 if side == 0 else -1.0
+            for k in range(fields):
+                for p in range(planes):
+                    slot = k * planes + p
+                    out_ref[k, p, row:row + 1, :] += (sign * inv_r[row:row + 1, :]) * rad_recv[side, slot:slot + 1, :]
 
     @pl.when(near)
     def _():
@@ -527,18 +561,6 @@
                         cb = jnp.broadcast_to(src_b[:, npack + u:npack + u + 1], (8, 128))
                         w = near_c[half, k, p, part, :] + spread[0, part, :] * cf + spread[1, part, :] * cb
                         out_ref[k, p, part, half * 128:(half + 1) * 128] = w
-
-    pl.when(rads[0][3])(lambda: answered(rad_ready.at[0], rad_copy(0).start))
-    for side in (0, 1):
-        @pl.when(rads[side][0])
-        def _():
-            rad_copy(1 - side).wait_recv()
-            row = 0 if side == 0 else rows - 1
-            sign = 1.0 if side == 0 else -1.0
-            for k in range(fields):
-                for p in range(planes):
-                    slot = k * planes + p
-                    out_ref[k, p, row:row + 1, :] += (sign * inv_r[row:row + 1, :]) * rad_recv[side, slot:slot + 1, :]
 
     @pl.when(near)
     def _():
@@ -582,8 +604,8 @@
             pltpu.VMEM((2, 8, 128), f32),
             pltpu.VMEM((len(SHIFTS), NEAR, 128), f32),
             pltpu.VMEM((len(SHIFTS), NEAR, 128), f32),
-            pltpu.VMEM((NEAR, cells), f32),
-            pltpu.VMEM((NEAR, cells), f32),
+            pltpu.VMEM((3, NEAR, cells), f32),
+            pltpu.VMEM((3, NEAR, cells), f32),
             pltpu.VMEM((3, NEAR, 128), f32),
             pltpu.VMEM((8, 128), f32),
             pltpu.VMEM((3, nsec, 8, 128), f32),

time: 14.5 us -> 14.3 us (0.986)
  the two profiles are of different devices: /device:TPU:57 before, /device:TPU:1 now
where the time goes in v6:
time: 14.3 us; the launch traced here: 14.1 us
  Pallas kernels  13.3 us (93%)
  local copies, waits for them, and re-layouts  0.84 us (6%)
    pallas_call x1, Pallas kernels, body(): pl.pallas_call(functools.partial(kernel, nsec, nrad, nax), out_shape=pltp...  13.3 us
    unnamed x1, local copies, waits for them, and re-layouts  0.84 us

profile of v6, /device:TPU:1, one launch (start us, length us, event | category | flops | bytes accessed | tf_op | source)
XLA Modules:
  0.0 14.1 jit_solution(8272044049627706191)
XLA Ops:
  0.0 13.3 %shard_map.28 = f32[5,2,64,256]{3,2,1,0:T(8,128)S(1)} custom-call(s32[16]{0:T(128)} %coarsen_hbm.1, f32[5,2,64,256]{3,2,1,0:T(8,128)} %state_ref.1), custom_call_target="tpu_custom_call" | custom-call | flops 4000000 | bytes 2000000 | tf_op jit(solution)/shard_map/pallas_call | solution.py:585
  13.3 0.8 %copy.4 = f32[5,2,64,256]{3,2,1,0:T(8,128)} copy(f32[5,2,64,256]{3,2,1,0:T(8,128)S(1)} %shard_map.28) | data formatting | bytes 1310720

commit v7 on v6

--- a/solution.py
+++ b/solution.py
@@ -139,6 +139,59 @@
 
     visit("greet", lambda to, s, a: signal(barrier, {"sec": s, "ax": a}))
     pl.when(reach)(lambda: signal(barrier, {"sec": 0, "ax": 0}))
+
+    def ax_copy(side, c):
+        part = pl.ds(c * crow, crow)
+        return pltpu.make_async_remote_copy(
+            src_ref=state_ref.at[:, (planes - 1) if side == 1 else 0, part, :],
+            dst_ref=ghost.at[1 - side, :, part, :],
+            send_sem=ax_ssem.at[side, c],
+            recv_sem=ax_rsem.at[1 - side, c],
+            device_id=sides[side][1],
+            device_id_type=MESH,
+        )
+
+    def answered(ready, send):
+        pl.semaphore_wait(ready, 1)
+        send()
+
+    def send_ax(side, chunks):
+        for c in chunks:
+            ax_copy(side, c).start()
+
+    odd = ax % 2
+
+    def enter():
+        def number(flags):
+            return sum(jnp.where(flag, 1, 0) for flag in flags)
+
+        count = number(v[2] for v in rads + sides)
+        count = count + jnp.where(near, sum(size(to, "early") for to in range(3)), number(v[2] for v in secs))
+        pl.when(count > 0)(lambda: pl.semaphore_wait(barrier, count))
+
+        for ready, pairs in ((ax_ready, sides), (sec_ready, secs), (rad_ready, rads)):
+            for side in (0, 1):
+                pl.when(pairs[side][2])(functools.partial(signal, ready.at[1 - side], pairs[side][1]))
+
+        for side in (0, 1):
+            pl.when(sides[side][2] & (odd != side))(functools.partial(send_ax, side, range(CHUNKS)))
+        def answer(t, carry):
+            s = jnp.where(t < nsec // 2, t, nsec + nsec // 2 - 1 - t)
+            for to in (1, 0, 2):
+                pl.when(there(to) & (t >= spans(to, "answer")[0][0]))(
+                    functools.partial(signal, packet_ready.at[jnp.where(tardy, 1, 0)], {"sec": s, "ax": ax + (to - 1)})
+                )
+            return carry
+
+        @pl.when(near)
+        def _():
+            for lo, hi in ((0, spans(1, "answer")[0][1]), spans(1, "answer")[1]):
+                lax.fori_loop(lo, hi, answer, 0)
+
+        for side in (0, 1):
+            pl.when(sides[side][2] & (odd == side))(functools.partial(send_ax, side, range(CHUNKS)))
+
+    pl.when(tardy)(enter)
 
     lane = lax.broadcasted_iota(jnp.int32, (8, 128), 1)
     consts = filter_constants(total)
@@ -268,42 +321,8 @@
         place = rad * rows + lax.broadcasted_iota(jnp.int32, (size, cells), 0)
         return 1.0 / (place.astype(jnp.float32) + 0.5)
 
-    def number(flags):
-        return sum(jnp.where(flag, 1, 0) for flag in flags)
-
-    count = number(v[2] for v in rads + sides)
-    count = count + jnp.where(near, sum(size(to, "early") for to in range(3)), number(v[2] for v in secs))
-    pl.when(count > 0)(lambda: pl.semaphore_wait(barrier, count))
-
-    for ready, pairs in ((ax_ready, sides), (sec_ready, secs), (rad_ready, rads)):
-        for side in (0, 1):
-            pl.when(pairs[side][2])(functools.partial(signal, ready.at[1 - side], pairs[side][1]))
-
-    def ax_copy(side, c):
-        part = pl.ds(c * crow, crow)
-        return pltpu.make_async_remote_copy(
-            src_ref=state_ref.at[:, (planes - 1) if side == 1 else 0, part, :],
-            dst_ref=ghost.at[1 - side, :, part, :],
-            send_sem=ax_ssem.at[side, c],
-            recv_sem=ax_rsem.at[1 - side, c],
-            device_id=sides[side][1],
-            device_id_type=MESH,
-        )
-
-    def answered(ready, send):
-        pl.semaphore_wait(ready, 1)
-        send()
-
-    def send_ax(side, chunks):
-        for c in chunks:
-            ax_copy(side, c).start()
-
-    odd = ax % 2
-    for side in (0, 1):
-        pl.when(sides[side][2] & (odd != side))(functools.partial(send_ax, side, range(CHUNKS)))
-    visit("answer", lambda to, s, a: signal(packet_ready.at[jnp.where(tardy, 1, 0)], {"sec": s, "ax": a}))
-    for side in (0, 1):
-        pl.when(sides[side][2] & (odd == side))(functools.partial(send_ax, side, range(CHUNKS)))
+    pl.when(~tardy)(enter)
+
     @pl.when(near)
     def _():
         pack = zero

time: 14.3 us -> 14.2 us (level)
  no operation moved by 1% of the time
where the time goes in v7:
time: 14.2 us; the launch traced here: 14.1 us
  Pallas kernels  13.2 us (93%)
  local copies, waits for them, and re-layouts  0.84 us (6%)
    pallas_call x1, Pallas kernels, body(): pl.pallas_call(functools.partial(kernel, nsec, nrad, nax), out_shape=pltp...  13.2 us
    unnamed x1, local copies, waits for them, and re-layouts  0.84 us

profile of v7, /device:TPU:1, one launch (start us, length us, event | category | flops | bytes accessed | tf_op | source)
XLA Modules:
  0.0 14.1 jit_solution(5454014614387610152)
XLA Ops:
  0.0 13.2 %shard_map.28 = f32[5,2,64,256]{3,2,1,0:T(8,128)S(1)} custom-call(s32[16]{0:T(128)} %coarsen_hbm.1, f32[5,2,64,256]{3,2,1,0:T(8,128)} %state_ref.1), custom_call_target="tpu_custom_call" | custom-call | flops 4000000 | bytes 2000000 | tf_op jit(solution)/shard_map/pallas_call | solution.py:604
  13.3 0.8 %copy.4 = f32[5,2,64,256]{3,2,1,0:T(8,128)} copy(f32[5,2,64,256]{3,2,1,0:T(8,128)S(1)} %shard_map.28) | data formatting | bytes 1310720

commit v8 on v7

--- a/solution.py
+++ b/solution.py
@@ -452,15 +452,6 @@
 
     pl.when(rads[1][3])(lambda: answered(rad_ready.at[1], rad_copy(1).start))
 
-    @pl.when(near)
-    def _():
-        for side in (0, 1):
-            pl.when(sides[side][3] & ~sides[side][4])(functools.partial(packet_to, 2 * side, sec, ax + 2 * side - 1))
-        answers = sum(size(to, "late") for to in range(3))
-        pl.when(answers > 0)(lambda: pl.semaphore_wait(packet_ready.at[0], answers))
-
-    visit("late", packet_to)
-
     def axial(c, both=(0, 1)):
         for side in both:
             @pl.when(sides[side][0])
@@ -500,8 +491,24 @@
                         keeps = jnp.where(lane == npack + u, head, keeps)
         keep_ref[...] = keeps if p == planes - 1 else keep_ref[...] + keeps
 
-    axial(0, (1,))
-    pl.when(near)(functools.partial(scan, 1))
+    earliest = near & (turn == 0)
+
+    def second_plane():
+        axial(0, (1,))
+        pl.when(near)(functools.partial(scan, 1))
+
+    pl.when(earliest)(second_plane)
+
+    @pl.when(near)
+    def _():
+        for side in (0, 1):
+            pl.when(sides[side][3] & ~sides[side][4])(functools.partial(packet_to, 2 * side, sec, ax + 2 * side - 1))
+        answers = sum(size(to, "late") for to in range(3))
+        pl.when(answers > 0)(lambda: pl.semaphore_wait(packet_ready.at[0], answers))
+
+    visit("late", packet_to)
+
+    pl.when(~earliest)(second_plane)
 
     @pl.when(sides[0][4])
     def _():

time: 14.2 us -> 14.2 us (level)
  no operation moved by 1% of the time
where the time goes in v8:
time: 14.2 us; the launch traced here: 14.1 us
  Pallas kernels  13.2 us (93%)
  local copies, waits for them, and re-layouts  0.84 us (6%)
    pallas_call x1, Pallas kernels, body(): pl.pallas_call(functools.partial(kernel, nsec, nrad, nax), out_shape=pltp...  13.2 us
    unnamed x1, local copies, waits for them, and re-layouts  0.84 us

profile of v8, /device:TPU:1, one launch (start us, length us, event | category | flops | bytes accessed | tf_op | source)
XLA Modules:
  0.0 14.1 jit_solution(4364475857984220380)
XLA Ops:
  0.0 13.2 %shard_map.28 = f32[5,2,64,256]{3,2,1,0:T(8,128)S(1)} custom-call(s32[16]{0:T(128)} %coarsen_hbm.1, f32[5,2,64,256]{3,2,1,0:T(8,128)} %state_ref.1), custom_call_target="tpu_custom_call" | custom-call | flops 4000000 | bytes 2000000 | tf_op jit(solution)/shard_map/pallas_call | solution.py:611
  13.3 0.8 %copy.4 = f32[5,2,64,256]{3,2,1,0:T(8,128)} copy(f32[5,2,64,256]{3,2,1,0:T(8,128)S(1)} %shard_map.28) | data formatting | bytes 1310720

commit v9 on v6

--- a/solution.py
+++ b/solution.py
@@ -301,7 +301,19 @@
     odd = ax % 2
     for side in (0, 1):
         pl.when(sides[side][2] & (odd != side))(functools.partial(send_ax, side, range(CHUNKS)))
-    visit("answer", lambda to, s, a: signal(packet_ready.at[jnp.where(tardy, 1, 0)], {"sec": s, "ax": a}))
+    def answer(t, carry):
+        s = jnp.where(t < nsec // 2, t, nsec + nsec // 2 - 1 - t)
+        for to in (1, 0, 2):
+            pl.when(there(to) & (t >= spans(to, "answer")[0][0]))(
+                functools.partial(signal, packet_ready.at[jnp.where(tardy, 1, 0)], {"sec": s, "ax": ax + (to - 1)})
+            )
+        return carry
+
+    @pl.when(near)
+    def _():
+        for lo, hi in ((0, spans(1, "answer")[0][1]), spans(1, "answer")[1]):
+            lax.fori_loop(lo, hi, answer, 0)
+
     for side in (0, 1):
         pl.when(sides[side][2] & (odd == side))(functools.partial(send_ax, side, range(CHUNKS)))
     @pl.when(near)

time: 14.3 us -> 14.3 us (level)
  no operation moved by 1% of the time
where the time goes in v9:
time: 14.3 us; the launch traced here: 14.1 us
  Pallas kernels  13.3 us (93%)
  local copies, waits for them, and re-layouts  0.84 us (6%)
    pallas_call x1, Pallas kernels, body(): pl.pallas_call(functools.partial(kernel, nsec, nrad, nax), out_shape=pltp...  13.3 us
    unnamed x1, local copies, waits for them, and re-layouts  0.84 us

profile of v9, /device:TPU:1, one launch (start us, length us, event | category | flops | bytes accessed | tf_op | source)
XLA Modules:
  0.0 14.1 jit_solution(9108699669363390292)
XLA Ops:
  0.0 13.3 %shard_map.28 = f32[5,2,64,256]{3,2,1,0:T(8,128)S(1)} custom-call(s32[16]{0:T(128)} %coarsen_hbm.1, f32[5,2,64,256]{3,2,1,0:T(8,128)} %state_ref.1), custom_call_target="tpu_custom_call" | custom-call | flops 4000000 | bytes 2000000 | tf_op jit(solution)/shard_map/pallas_call | solution.py:597
  13.3 0.8 %copy.4 = f32[5,2,64,256]{3,2,1,0:T(8,128)} copy(f32[5,2,64,256]{3,2,1,0:T(8,128)S(1)} %shard_map.28) | data formatting | bytes 1310720
